TPU v7x, 32 devices: a whole 2x2x4 slice. The times are simulated.
32 devices in a mesh: phase: 4 (over x, core), dp: 8 (over z, y).
Axes of the slice: x: 2, y: 2, z: 4, core: 2. Of those that a mesh axis runs over, the one named last changes fastest.
Arguments:
- features: bfloat16 [2, 131072], P(None, 'dp'), may hold values from -40 to 40
- site_counts: int32 [2, 8], P(None, 'dp'), may hold values from 16 to 256, as said below
- kernel_map_0: int32 [2, 27, 2048], P(None, None, 'dp'), may hold values from -1 to 255, as said below
- kernel_map_1: int32 [2, 27, 1024], P(None, None, 'dp'), may hold values from -1 to 127, as said below
- kernel_map_2: int32 [2, 27, 512], P(None, None, 'dp'), may hold values from -1 to 63, as said below
- kernel_map_3: int32 [2, 27, 256], P(None, None, 'dp'), may hold values from -1 to 31, as said below
- parent_map_0: int32 [2, 2048], P(None, 'dp'), may hold values from -1 to 127, as said below
- parent_map_1: int32 [2, 1024], P(None, 'dp'), may hold values from -1 to 63, as said below
- parent_map_2: int32 [2, 512], P(None, 'dp'), may hold values from -1 to 31, as said below
- depthwise_0: bfloat16 [27, 64], replicated, may hold values from -1.5 to 1.5
- depthwise_1: bfloat16 [27, 128], replicated, may hold values from -1.5 to 1.5
- depthwise_2: bfloat16 [27, 256], replicated, may hold values from -1.5 to 1.5
- depthwise_3: bfloat16 [27, 512], replicated, may hold values from -1.5 to 1.5
- first_weight_0: bfloat16 [64, 64], replicated, may hold values from -0.75 to 0.75
- first_weight_1: bfloat16 [128, 128], replicated, may hold values from -0.5 to 0.5
- first_weight_2: bfloat16 [256, 256], replicated, may hold values from -0.375 to 0.375
- first_weight_3: bfloat16 [512, 512], replicated, may hold values from -0.25 to 0.25
- second_weight_0: bfloat16 [64, 64], replicated, may hold values from -0.75 to 0.75
- second_weight_1: bfloat16 [128, 128], replicated, may hold values from -0.5 to 0.5
- second_weight_2: bfloat16 [256, 256], replicated, may hold values from -0.375 to 0.375
- second_weight_3: bfloat16 [512, 512], replicated, may hold values from -0.25 to 0.25
- coarsen_0: bfloat16 [64, 128], replicated, may hold values from -0.75 to 0.75
- coarsen_1: bfloat16 [128, 256], replicated, may hold values from -0.5 to 0.5
- coarsen_2: bfloat16 [256, 512], replicated, may hold values from -0.375 to 0.375
- refine_0: bfloat16 [128, 64], replicated, may hold values from -0.5 to 0.5
- refine_1: bfloat16 [256, 128], replicated, may hold values from -0.375 to 0.375
- refine_2: bfloat16 [512, 256], replicated, may hold values from -0.25 to 0.25
- cotangent: bfloat16 [4, 2, 131072], P('phase', None, 'dp'), may hold values from -6 to 6
Outputs:
- decoded: bfloat16 [4, 2, 131072], P('phase', None, 'dp')
- weight_grads: float32 [4, 2, 262144], P('phase', None, 'dp')
Inputs may be any that keep to these rules, and one draw needn't show every extreme that they name: `site_counts`: live finest-level sites of a replica in a micro-batch; in every micro-batch some replica has all 256 slots live. `kernel_map_0`: row index within the same replica's block, or -1 for no neighbour; live sites come first in each block, a live site's offset 13 names itself, live sites name only live sites, padded rows hold -1. `kernel_map_1`: as for level 0, at level 1. `kernel_map_2`: as for level 0, at level 2. `kernel_map_3`: as for level 0, at level 3. `parent_map_0`: a live level 1 site of the same replica and micro-batch, -1 for padded rows. `parent_map_1`: a live level 2 site of the same replica and micro-batch, -1 for padded rows. `parent_map_2`: a live level 3 site of the same replica and micro-batch, -1 for padded rows.
All inputs are finite; a program needn't handle non-finite values.
Results may differ from a plain program's by a relative error of at most 0.014.
Values may be sent and summed in bfloat16 or wider, within the bound.
A program may use at most 256 MiB of HBM per device.

v0:
```python
import functools
import math

import jax
import jax.numpy as jnp
from jax import lax
from jax.experimental import pallas as pl
from jax.experimental.pallas import tpu as pltpu
from jax.sharding import PartitionSpec as P

LANES = 128
TAPS = 27
IDX_ROWS = 32
BATCH = 9
F32 = jnp.float32
BF16 = jnp.bfloat16
MESH = pl.DeviceIdType.MESH
GELU_A = math.sqrt(2.0 / math.pi)
GELU_B = 0.044715


def dot(a, b):
    return lax.dot_general(a, b, (((1,), (0,)), ((), ())), preferred_element_type=F32)


def dot_nt(a, b):
    return lax.dot_general(a, b, (((1,), (1,)), ((), ())), preferred_element_type=F32)


def dot_tn(a, b):
    return lax.dot_general(a, b, (((0,), (0,)), ((), ())), preferred_element_type=F32)


def one_hot(column, width):
    lanes = lax.broadcasted_iota(jnp.int32, (column.shape[0], width), 1).astype(F32)
    return jnp.where(column == lanes, 1.0, 0.0).astype(BF16)


def pool_matrix(parent_row, coarse):
    rows = lax.broadcasted_iota(jnp.int32, (coarse, parent_row.shape[1]), 0)
    return jnp.where(rows == parent_row, 1.0, 0.0).astype(F32)


def kernel(replicas, heights, widths, micro, count, *refs):
    sources, (dec_out, grad_out) = refs[:count], refs[count : count + 2]
    held, refs = refs[count + 2 : 2 * count + 2], refs[2 * count + 2 :]
    (
        load_sem,
        pack_f,
        pack_c,
        pack_d,
        pack_g,
        small,
        idx_raw,
        idx,
        idx_t,
        part0,
        part1,
        part2,
        got0,
        got1,
        got2,
        near0,
        near1,
        near2,
        sum0,
        sum1,
        sum2,
        cot_all,
        slope_all,
        cols_send,
        cols_all,
        send_part,
        recv_part,
        send_cot,
        recv_cot,
        send_slope,
        recv_slope,
        send_cols,
        recv_cols,
        send_near,
        recv_near,
    ) = refs
    nears, sums_of = (near0, near1, near2), (sum0, sum1, sum2)
    features, counts, cot = held[0], held[1], held[27]
    kms, pms, dws = held[2:6], held[6:9], held[9:13]
    fws, sws = held[13:17], held[17:21]
    cos, res = held[21:24], held[24:27]
    parts, gots = (part0, part1, part2), (got0, got1, got2)
    phase = lax.axis_index("phase")
    me = lax.axis_index("dp")
    chunks = features.shape[1] // LANES

    def peer(offset):
        return {"phase": phase, "dp": lax.rem(me + offset, replicas)}

    def load(i):
        return pltpu.make_async_copy(sources[i], held[i], load_sem.at[i])

    order = [0, 27, 2, 3, 4, 5, 6, 7, 8, 1, 9, 13, 17, 21, 10, 14, 18, 22, 11, 15, 19, 23, 12, 16, 20]
    for i in order + [26, 25, 24]:
        load(i).start()

    barrier = pltpu.get_barrier_semaphore()

    @pl.loop(1, replicas)
    def _(offset):
        pl.semaphore_signal(barrier, inc=1, device_id=peer(offset), device_id_type=MESH)

    for i in (0, 27):
        load(i).wait()

    for j in range(chunks):
        lanes = slice(j * LANES, (j + 1) * LANES)
        pack_f[2 * j : 2 * j + 2, :] = features[:, lanes].astype(F32)
        pack_c[2 * j : 2 * j + 2, :] = cot[0, :, lanes].astype(F32)

    def unpack(pack, layer, m):
        rows, width = heights[layer], widths[layer]
        if width < LANES:
            both = pack[pl.ds(m, rows // 2, stride=2), :]
            small[pl.ds(0, rows // 2, stride=2), :] = both[:, :width]
            small[pl.ds(1, rows // 2, stride=2), :] = both[:, width:]
            return small[...]
        split = width // LANES
        return jnp.concatenate(
            [pack[pl.ds(2 * h + m, rows, stride=2 * split), :] for h in range(split)], axis=1
        )

    def target(layer):
        return jnp.concatenate([unpack(pack_c, layer, m) for m in range(micro)], axis=0).astype(BF16)

    top = 3

    pl.semaphore_wait(barrier, replicas - 1)

    def all_send(source, gathered, send_sem, recv_sem, indexed):
        def copy(offset):
            to = peer(offset)
            return pltpu.make_async_remote_copy(
                src_ref=source.at[to["dp"]] if indexed else source.at[0],
                dst_ref=gathered.at[offset],
                send_sem=send_sem.at[offset],
                recv_sem=recv_sem.at[offset],
                device_id=to,
                device_id_type=MESH,
            )

        return copy

    copy_cot = all_send(cot_all, cot_all, send_cot, recv_cot, False)
    copy_slope = all_send(slope_all, slope_all, send_slope, recv_slope, False)
    copy_cols = all_send(cols_send, cols_all, send_cols, recv_cols, True)

    def start_all(copy):
        @pl.loop(1, replicas)
        def _(offset):
            copy(offset).start()

    def wait_all(copy):
        @pl.loop(1, replicas)
        def _(offset):
            copy(offset).wait()

    def group_of(layer):
        owners = parts[layer].shape[0]
        return owners, lax.div(me, owners), lax.rem(me, owners)

    def near_copy(layer, w, sender):
        owners, group, _ = group_of(layer)
        return pltpu.make_async_remote_copy(
            src_ref=parts[layer].at[w],
            dst_ref=nears[layer].at[sender],
            send_sem=send_near.at[w],
            recv_sem=recv_near.at[sender],
            device_id={"phase": phase, "dp": group * owners + w},
            device_id_type=MESH,
        )

    def far_copy(layer, group):
        return pltpu.make_async_remote_copy(
            src_ref=sums_of[layer].at[0],
            dst_ref=gots[layer].at[group],
            send_sem=send_part.at[0],
            recv_sem=recv_part.at[group],
            device_id={"phase": phase, "dp": group_of(layer)[2]},
            device_id_type=MESH,
        )

    @pl.when(phase == top)
    def _():
        cot_all[0] = target(top)
        start_all(copy_cot)

    for i in (2, 3, 4, 5, 6, 7, 8, 1):
        load(i).wait()
    idx[...] = jnp.full(idx.shape, -1.0, F32)
    base = []
    position = 0
    for layer in range(4):
        rows = heights[layer]
        base.append(position)
        pieces = [(at, min(LANES, rows - at)) for at in range(0, rows, LANES)]
        for k in range(TAPS):
            for piece, (at, span) in enumerate(pieces):
                idx_raw[piece, 2 * k : 2 * k + 2, 0:span] = kms[layer][k, :, at : at + span].astype(F32)
        for m in range(micro):
            at = position + m * rows
            values = jnp.concatenate(
                [
                    idx_raw.at[piece][pl.ds(m, TAPS, stride=2), :][:, :span]
                    for piece, (_, span) in enumerate(pieces)
                ],
                axis=1,
            )
            shift = m * rows if layer >= 2 else 0
            if shift:
                values = jnp.where(values < 0.0, values, values + float(shift))
            idx[0:TAPS, at : at + rows] = values
            if layer < 3:
                idx[TAPS : TAPS + 1, at : at + rows] = pms[layer][m : m + 1, :].astype(F32)
        position += micro * rows
    for j in range(idx.shape[1] // LANES):
        lanes = slice(j * LANES, (j + 1) * LANES)
        idx_t[lanes, :] = idx[:, lanes].T

    live = []
    for m in range(micro):
        block = unpack(pack_f, 0, m)
        site = lax.broadcasted_iota(jnp.int32, block.shape, 0)
        live.append(jnp.where(site < counts[:, m : m + 1], block, 0.0))
    x = jnp.concatenate(live, axis=0).astype(BF16)

    encodes = []
    for layer in range(4):
        for i in (9 + layer, 13 + layer, 17 + layer) + ((21 + layer,) if layer < 3 else ()):
            load(i).wait()
        rows, width = heights[layer], widths[layer]
        group = rows if layer < 2 else micro * rows
        mixes = []
        for start in range(0, micro * rows, group):
            block = x[start : start + group]
            index = idx_t[base[layer] + start : base[layer] + start + group, :]
            mixed = jnp.zeros((group, width), F32)
            for first in range(0, TAPS, BATCH):
                hots = [one_hot(index[:, k : k + 1], group) for k in range(first, first + BATCH)]
                gathered = dot(jnp.concatenate(hots, axis=0), block)
                for k in range(BATCH):
                    tap = dws[layer][first + k : first + k + 1, :].astype(F32)
                    mixed = mixed + gathered[k * group : (k + 1) * group] * tap
            mixes.append(mixed)
        mixed = mixes[0] if len(mixes) == 1 else jnp.concatenate(mixes, axis=0)
        normed_f = mixed * lax.rsqrt(jnp.mean(mixed * mixed, axis=1, keepdims=True) + 1e-05)
        normed = normed_f.astype(BF16)
        inner = dot(normed, fws[layer][...])
        squared = inner * inner
        bend = jnp.tanh(GELU_A * inner * (1.0 + GELU_B * squared))
        active = (0.5 * inner * (1.0 + bend)).astype(BF16)
        encoded = (x.astype(F32) + dot(active, sws[layer][...])).astype(BF16)
        encodes.append(encoded)

        @pl.when(phase == layer)
        def _():
            aim = target(layer) if layer < top else cot_all[0]
            backward = dot_nt(aim, sws[layer][...])
            grad = 0.5 * (1.0 + bend) + 0.5 * inner * (1.0 - bend * bend) * GELU_A * (
                1.0 + 3.0 * GELU_B * squared
            )
            slope = (grad * backward).astype(BF16)
            if layer == top:
                slope_all[0] = slope
                both = jnp.concatenate(
                    [normed.astype(F32).T, active.astype(F32).T], axis=1
                ).astype(cols_send.dtype)
                rows_here = cols_send.shape[1]
                for d in range(replicas):
                    cols_send[d] = both[d * rows_here : (d + 1) * rows_here]
                start_all(copy_slope)
                start_all(copy_cols)
            else:
                part = parts[layer]
                owners, _, rows_here, _ = part.shape
                for i, term in enumerate((dot_tn(normed, slope), dot_tn(active, aim))):
                    for w in range(owners):
                        part[w, i] = term[w * rows_here : (w + 1) * rows_here].astype(part.dtype)
                for w in range(owners):

                    @pl.when(group_of(layer)[2] != w)
                    def _():
                        near_copy(layer, w, group_of(layer)[2]).start()

        if layer < 3:
            coarse = heights[layer + 1]
            pooled = []
            for m in range(micro):
                matrix = pool_matrix(pms[layer][m : m + 1, :], coarse)
                number = jnp.sum(matrix, axis=1, keepdims=True)
                sums = dot(matrix.astype(BF16), encoded[m * rows : (m + 1) * rows])
                pooled.append(sums / jnp.maximum(number, 1.0))
            x = dot(jnp.concatenate(pooled, axis=0).astype(BF16), cos[layer][...]).astype(BF16)

    for layer in range(3):
        part, near = parts[layer], nears[layer]

        @pl.when(phase == layer)
        def _():
            owners, group, member = group_of(layer)
            near[member] = part[member]
            for w in range(owners):

                @pl.when(member != w)
                def _():
                    near_copy(layer, w, member).wait_send()
                    near_copy(layer, w, w).wait_recv()

            for i in range(2):
                term = near[0, i].astype(F32)
                for w in range(1, owners):
                    term = term + near[w, i].astype(F32)
                sums_of[layer][0, i] = term.astype(near.dtype)

            @pl.when(group != 0)
            def _():
                far_copy(layer, group).start()

    decoded = encodes[3]
    for layer in range(3, -1, -1):
        rows, width = heights[layer], widths[layer]
        if layer < 3:
            coarse = heights[layer + 1]
            load(24 + layer).wait()
            mix = dot_nt if layer == 0 else dot
            lifted = mix(decoded, res[layer][...]).astype(BF16)
            ups = []
            for m in range(micro):
                at = base[layer] + m * rows
                matrix = one_hot(idx_t[at : at + rows, TAPS : TAPS + 1], coarse)
                ups.append(dot(matrix, lifted[m * coarse : (m + 1) * coarse]))
            decoded = (encodes[layer].astype(F32) + jnp.concatenate(ups, axis=0)).astype(BF16)

        @pl.when(phase == layer)
        def _():
            wide = decoded.astype(F32)
            for m in range(micro):
                own = wide[m * rows : (m + 1) * rows]
                if width < LANES:
                    small[...] = own
                    pack_d[pl.ds(m, rows // 2, stride=2), :] = jnp.concatenate(
                        [
                            small[pl.ds(0, rows // 2, stride=2), :],
                            small[pl.ds(1, rows // 2, stride=2), :],
                        ],
                        axis=1,
                    )
                else:
                    split = width // LANES
                    for h in range(split):
                        pack_d[pl.ds(2 * h + m, rows, stride=2 * split), :] = own[
                            :, h * LANES : (h + 1) * LANES
                        ]

    for j in range(chunks):
        dec_out[0, :, j * LANES : (j + 1) * LANES] = pack_d[2 * j : 2 * j + 2, :].astype(BF16)

    pack_g[...] = jnp.zeros(pack_g.shape, F32)

    def put_grad(layer, i, term):
        rows_here, width = term.shape
        term = term * (micro * replicas * heights[layer]) ** -0.5
        if width < LANES:
            small[0:rows_here, :] = term
            pack_g[pl.ds(i, rows_here // 2, stride=2), :] = jnp.concatenate(
                [
                    small[pl.ds(0, rows_here // 2, stride=2), :],
                    small[pl.ds(1, rows_here // 2, stride=2), :],
                ],
                axis=1,
            )
        else:
            split = width // LANES
            for h in range(split):
                pack_g[pl.ds(2 * h + i, rows_here, stride=2 * split), :] = term[
                    :, h * LANES : (h + 1) * LANES
                ]

    for layer in range(3):
        got = gots[layer]

        @pl.when(phase == layer)
        def _():
            owners, group, _ = group_of(layer)
            groups = replicas // owners

            @pl.when(group != 0)
            def _():
                far_copy(layer, group).wait_send()

            @pl.when(group == 0)
            def _():
                got[0] = sums_of[layer][0]
                for sender in range(1, groups):
                    far_copy(layer, sender).wait_recv()
                for i in range(2):
                    term = got[0, i].astype(F32)
                    for sender in range(1, groups):
                        term = term + got[sender, i].astype(F32)
                    put_grad(layer, i, term)

    @pl.when(phase == top)
    def _():
        wait_all(copy_cot)
        cols_all[0] = cols_send[me]
        wait_all(copy_cols)
        wait_all(copy_slope)
        span = micro * heights[top]

        def terms(slot):
            cols = cols_all[slot].astype(BF16)
            return (
                dot(cols[:, :span], slope_all[slot]),
                dot(cols[:, span:], cot_all[slot]),
            )

        total = terms(0)
        if replicas <= 16:
            for slot in range(1, replicas):
                total = jax.tree.map(jnp.add, total, terms(slot))
        else:
            total = lax.fori_loop(
                1, replicas, lambda s, t: jax.tree.map(jnp.add, t, terms(s)), total
            )
        for i in range(2):
            put_grad(top, i, total[i])

    for q in range(grad_out.shape[2] // LANES):
        grad_out[0, :, q * LANES : (q + 1) * LANES] = pack_g[2 * q : 2 * q + 2, :]


def on_device(*arrays):
    features, kms, dws = arrays[0], arrays[2:6], arrays[9:13]
    arrays = list(arrays)
    arrays[1] = arrays[1].T
    arrays[2:6] = [jnp.transpose(km, (1, 0, 2)) for km in kms]
    arrays[24] = arrays[24].T
    widths = [taps.shape[1] for taps in dws]
    heights = [km.shape[2] for km in kms]
    micro, elements = features.shape
    replicas = lax.axis_size("dp")
    owned = widths[3] * widths[3] // replicas

    def narrow(rows):
        return BF16 if rows % 16 == 0 else F32

    parts, gots, nears, sums_of = [], [], [], []
    for layer in range(3):
        rows_here = min(widths[layer], owned // widths[layer])
        owners = widths[layer] // rows_here
        kind = narrow(rows_here)
        parts.append(pltpu.VMEM((owners, 2, rows_here, widths[layer]), kind))
        gots.append(pltpu.VMEM((replicas // owners, 2, rows_here, widths[layer]), kind))
        nears.append(pltpu.VMEM((owners, 2, rows_here, widths[layer]), kind))
        sums_of.append(pltpu.VMEM((1, 2, rows_here, widths[layer]), kind))
    top_rows = owned // widths[3]
    span = micro * heights[3]
    idx_lanes = -(-micro * sum(heights) // LANES) * LANES
    sem = pltpu.SemaphoreType.DMA((replicas,))
    scratch = [
        *[pltpu.VMEM(a.shape, a.dtype) for a in arrays],
        pltpu.SemaphoreType.DMA((len(arrays),)),
        pltpu.VMEM((2 * elements // LANES, LANES), F32),
        pltpu.VMEM((2 * elements // LANES, LANES), F32),
        pltpu.VMEM((2 * elements // LANES, LANES), F32),
        pltpu.VMEM((2 * owned // LANES, LANES), F32),
        pltpu.VMEM((heights[0], widths[0]), F32),
        pltpu.VMEM((-(-heights[0] // LANES), 2 * IDX_ROWS, LANES), F32),
        pltpu.VMEM((IDX_ROWS, idx_lanes), F32),
        pltpu.VMEM((idx_lanes, IDX_ROWS), F32),
        *parts,
        *gots,
        *nears,
        *sums_of,
        pltpu.VMEM((replicas, span, widths[3]), BF16),
        pltpu.VMEM((replicas, span, widths[3]), BF16),
        pltpu.VMEM((replicas, top_rows, 2 * span), narrow(top_rows)),
        pltpu.VMEM((replicas, top_rows, 2 * span), narrow(top_rows)),
        *[sem] * 10,
    ]
    return pl.pallas_call(
        functools.partial(kernel, replicas, heights, widths, micro, len(arrays)),
        out_shape=(
            jax.ShapeDtypeStruct((1, micro, elements), BF16),
            jax.ShapeDtypeStruct((1, 2, owned), F32),
        ),
        in_specs=[pl.BlockSpec(memory_space=pltpu.HBM)] * len(arrays),
        out_specs=[pl.BlockSpec(memory_space=pltpu.VMEM)] * 2,
        scratch_shapes=scratch,
        compiler_params=pltpu.CompilerParams(
            collective_id=0, has_side_effects=True, vmem_limit_bytes=64 * 1024 * 1024 - 512 * 1024
        ),
    )(*arrays)


def solution(mesh):
    placed = (
        (P(None, "dp"), P(None, "dp"))
        + (P(None, None, "dp"),) * 4
        + (P(None, "dp"),) * 3
        + (P(),) * 18
        + (P("phase", None, "dp"),)
    )
    return jax.shard_map(
        on_device,
        mesh=mesh,
        in_specs=placed,
        out_specs=(P("phase", None, "dp"), P("phase", None, "dp")),
        check_vma=False,
    )
```

profile of v0, /device:TPU:3, one launch (start us, length us, event | category | flops | bytes accessed | tf_op | source)
XLA Modules:
  0.0 30.0 jit_solution(3810068801104789346)
XLA Ops:
  0.6 26.1 %shard_map.275 = (bf16[1,2,16384]{2,1,0:T(2,128)(2,1)}, f32[1,2,32768]{2,1,0:T(2,128)}) custom-call(bf16[2,16384]{1,0:T(2,128)(2,1)} %refs_0_.1, s32[1,2]{1,0:T(1,128)} %bitcast.11, s32[27,2,256]{2,1,0:T(2,128)} %bitcast.6, s32[27,2,128]{2,1,0:T(2,128)} %bitcast.7, s32[27,2,64]{2,1,0:T(2,128)} %bitcast.8, s32[27,2,32]{2,1,0:T(2,128)} %bitcast.9, ...), custom_call_target="tpu_custom_call" | custom-call | tf_op jit(solution)/shard_map/pallas_call | solution.py:488
  26.8 1.5 %copy.32 = bf16[1,2,16384]{2,1,0:T(2,128)(2,1)} copy(bf16[1,2,16384]{2,1,0:T(2,128)(2,1)} %get-tuple-element.4) | data formatting | bytes 131072
  28.3 1.7 %copy.33 = f32[1,2,32768]{2,1,0:T(2,128)} copy(f32[1,2,32768]{2,1,0:T(2,128)} %get-tuple-element.5) | data formatting | bytes 524288
where the time goes:
time: 30.2 us; the launch traced here: 30 us
  Pallas kernels  26.1 us (86%)
  local copies, waits for them, and re-layouts  3.18 us (11%)
  between operations  0.65 us (2%)
    pallas_call x1, Pallas kernels, on_device(): pl.pallas_call(functools.partial(kernel, replicas, heights, widths, micro...  26.1 us
    unnamed x2, local copies, waits for them, and re-layouts  3.18 us

commit v1 on v0

--- a/solution.py
+++ b/solution.py
@@ -436,6 +436,17 @@
         grad_out[0, :, q * LANES : (q + 1) * LANES] = pack_g[2 * q : 2 * q + 2, :]
 
 
+def deliver(dec_in, grad_in, dec_out, grad_out, sem):
+    copies = [
+        pltpu.make_async_copy(grad_in, grad_out, sem.at[0]),
+        pltpu.make_async_copy(dec_in, dec_out, sem.at[1]),
+    ]
+    for copy in copies:
+        copy.start()
+    for copy in copies:
+        copy.wait()
+
+
 def on_device(*arrays):
     features, kms, dws = arrays[0], arrays[2:6], arrays[9:13]
     arrays = list(arrays)
@@ -485,11 +496,11 @@
         pltpu.VMEM((replicas, top_rows, 2 * span), narrow(top_rows)),
         *[sem] * 10,
     ]
-    return pl.pallas_call(
+    held = pl.pallas_call(
         functools.partial(kernel, replicas, heights, widths, micro, len(arrays)),
         out_shape=(
-            jax.ShapeDtypeStruct((1, micro, elements), BF16),
-            jax.ShapeDtypeStruct((1, 2, owned), F32),
+            pltpu.VMEM((1, micro, elements), BF16),
+            pltpu.VMEM((1, 2, owned), F32),
         ),
         in_specs=[pl.BlockSpec(memory_space=pltpu.HBM)] * len(arrays),
         out_specs=[pl.BlockSpec(memory_space=pltpu.VMEM)] * 2,
@@ -498,6 +509,17 @@
             collective_id=0, has_side_effects=True, vmem_limit_bytes=64 * 1024 * 1024 - 512 * 1024
         ),
     )(*arrays)
+    return pl.pallas_call(
+        deliver,
+        out_shape=(
+            jax.ShapeDtypeStruct((1, micro, elements), BF16),
+            jax.ShapeDtypeStruct((1, 2, owned), F32),
+        ),
+        in_specs=[pl.BlockSpec(memory_space=pltpu.VMEM)] * 2,
+        out_specs=[pl.BlockSpec(memory_space=pltpu.HBM)] * 2,
+        scratch_shapes=[pltpu.SemaphoreType.DMA((2,))],
+        compiler_params=pltpu.CompilerParams(vmem_limit_bytes=1024 * 1024),
+    )(*[pltpu.with_memory_space_constraint(a, pltpu.VMEM) for a in held])
 
 
 def solution(mesh):

time: 30.2 us -> 27 us (0.89)
  local copies, waits for them, and re-layouts: 3.18 us -> 0 us
    unnamed x2 -> x0, local copies, waits for them, and re-layouts: 3.18 us -> none
    pallas_call x0 -> x1, Pallas kernels: none -> 0.73 us  [on_device(): pl.pallas_call(deliver, out_shape=(jax.ShapeDtypeStruct((1, micro, elemen...]
    pallas_call x1, Pallas kernels: 26.1 us -> 25.5 us  [on_device(): pl.pallas_call(functools.partial(kernel, replicas, heights, widths, micro...]
where the time goes in v1:
time: 27 us; the launch traced here: 26.9 us
  Pallas kernels  26.2 us (97%)
  between operations  0.65 us (2%)
    pallas_call x1, Pallas kernels, on_device(): pl.pallas_call(functools.partial(kernel, replicas, heights, widths, micro...  25.5 us
    pallas_call x1, Pallas kernels, on_device(): pl.pallas_call(deliver, out_shape=(jax.ShapeDtypeStruct((1, micro, elemen...  0.73 us

profile of v1, /device:TPU:3, one launch (start us, length us, event | category | flops | bytes accessed | tf_op | source)
XLA Modules:
  0.0 26.9 jit_solution(4065332583992949190)
XLA Ops:
  0.6 25.5 %shard_map.275 = (bf16[1,2,16384]{2,1,0:T(2,128)(2,1)S(1)}, f32[1,2,32768]{2,1,0:T(2,128)S(1)}) custom-call(bf16[2,16384]{1,0:T(2,128)(2,1)} %refs_0_.1, s32[1,2]{1,0:T(1,128)} %bitcast.11, s32[27,2,256]{2,1,0:T(2,128)} %bitcast.6, s32[27,2,128]{2,1,0:T(2,128)} %bitcast.7, s32[27,2,64]{2,1,0:T(2,128)} %bitcast.8, s32[27,2,32]{2,1,0:T(2,128)} %bitcast.9, ...), custom_call_target="tpu_custom_call" | custom-call | tf_op jit(solution)/shard_map/pallas_call | solution.py:499
  26.1 0.7 %shard_map.276 = (bf16[1,2,16384]{2,1,0:T(2,128)(2,1)}, f32[1,2,32768]{2,1,0:T(2,128)}) custom-call(bf16[1,2,16384]{2,1,0:T(2,128)(2,1)S(1)} %get-tuple-element.4.dec_in, f32[1,2,32768]{2,1,0:T(2,128)S(1)} %get-tuple-element.5.grad_in), custom_call_target="tpu_custom_call" | custom-call | tf_op jit(solution)/shard_map/pallas_call | solution.py:512

commit v2 on v1

--- a/solution.py
+++ b/solution.py
@@ -132,17 +132,14 @@
 
     top = 3
 
-    pl.semaphore_wait(barrier, replicas - 1)
-
     def all_send(source, gathered, send_sem, recv_sem, indexed):
-        def copy(offset):
-            to = peer(offset)
+        def copy(to, sender):
             return pltpu.make_async_remote_copy(
-                src_ref=source.at[to["dp"]] if indexed else source.at[0],
-                dst_ref=gathered.at[offset],
-                send_sem=send_sem.at[offset],
-                recv_sem=recv_sem.at[offset],
-                device_id=to,
+                src_ref=source.at[to] if indexed else source.at[sender],
+                dst_ref=gathered.at[sender],
+                send_sem=send_sem.at[to],
+                recv_sem=recv_sem.at[sender],
+                device_id={"phase": phase, "dp": to},
                 device_id_type=MESH,
             )
 
@@ -152,15 +149,12 @@
     copy_slope = all_send(slope_all, slope_all, send_slope, recv_slope, False)
     copy_cols = all_send(cols_send, cols_all, send_cols, recv_cols, True)
 
-    def start_all(copy):
-        @pl.loop(1, replicas)
-        def _(offset):
-            copy(offset).start()
-
-    def wait_all(copy):
-        @pl.loop(1, replicas)
-        def _(offset):
-            copy(offset).wait()
+    def others(body):
+        @pl.loop(0, replicas)
+        def _(other):
+            @pl.when(other != me)
+            def _():
+                body(other)
 
     def group_of(layer):
         owners = parts[layer].shape[0]
@@ -189,8 +183,7 @@
 
     @pl.when(phase == top)
     def _():
-        cot_all[0] = target(top)
-        start_all(copy_cot)
+        cot_all[me] = target(top)
 
     for i in (2, 3, 4, 5, 6, 7, 8, 1):
         load(i).wait()
@@ -231,6 +224,30 @@
         live.append(jnp.where(site < counts[:, m : m + 1], block, 0.0))
     x = jnp.concatenate(live, axis=0).astype(BF16)
 
+    def pass_on(layer):
+        part, near = parts[layer], nears[layer]
+
+        @pl.when(phase == layer)
+        def _():
+            owners, group, member = group_of(layer)
+            near[member] = part[member]
+            for w in range(owners):
+
+                @pl.when(member != w)
+                def _():
+                    near_copy(layer, w, member).wait_send()
+                    near_copy(layer, w, w).wait_recv()
+
+            for i in range(2):
+                term = near[0, i].astype(F32)
+                for w in range(1, owners):
+                    term = term + near[w, i].astype(F32)
+                sums_of[layer][0, i] = term.astype(near.dtype)
+
+            @pl.when(group != 0)
+            def _():
+                far_copy(layer, group).start()
+
     encodes = []
     for layer in range(4):
         for i in (9 + layer, 13 + layer, 17 + layer) + ((21 + layer,) if layer < 3 else ()):
@@ -258,25 +275,36 @@
         active = (0.5 * inner * (1.0 + bend)).astype(BF16)
         encoded = (x.astype(F32) + dot(active, sws[layer][...])).astype(BF16)
         encodes.append(encoded)
+        if layer == 0:
+            pl.semaphore_wait(barrier, replicas - 1)
+
+            @pl.when(phase == top)
+            def _():
+                others(lambda to: copy_cot(to, me).start())
 
         @pl.when(phase == layer)
         def _():
-            aim = target(layer) if layer < top else cot_all[0]
+            aim = target(layer) if layer < top else cot_all[me]
             backward = dot_nt(aim, sws[layer][...])
             grad = 0.5 * (1.0 + bend) + 0.5 * inner * (1.0 - bend * bend) * GELU_A * (
                 1.0 + 3.0 * GELU_B * squared
             )
             slope = (grad * backward).astype(BF16)
             if layer == top:
-                slope_all[0] = slope
+                slope_all[me] = slope
                 both = jnp.concatenate(
                     [normed.astype(F32).T, active.astype(F32).T], axis=1
                 ).astype(cols_send.dtype)
                 rows_here = cols_send.shape[1]
                 for d in range(replicas):
                     cols_send[d] = both[d * rows_here : (d + 1) * rows_here]
-                start_all(copy_slope)
-                start_all(copy_cols)
+                cols_all[me] = cols_send[me]
+
+                @others
+                def _(to):
+                    copy_cols(to, me).start()
+                    copy_slope(to, me).start()
+
             else:
                 part = parts[layer]
                 owners, _, rows_here, _ = part.shape
@@ -288,6 +316,9 @@
                     @pl.when(group_of(layer)[2] != w)
                     def _():
                         near_copy(layer, w, group_of(layer)[2]).start()
+
+        if layer > 0:
+            pass_on(layer - 1)
 
         if layer < 3:
             coarse = heights[layer + 1]
@@ -298,30 +329,6 @@
                 sums = dot(matrix.astype(BF16), encoded[m * rows : (m + 1) * rows])
                 pooled.append(sums / jnp.maximum(number, 1.0))
             x = dot(jnp.concatenate(pooled, axis=0).astype(BF16), cos[layer][...]).astype(BF16)
-
-    for layer in range(3):
-        part, near = parts[layer], nears[layer]
-
-        @pl.when(phase == layer)
-        def _():
-            owners, group, member = group_of(layer)
-            near[member] = part[member]
-            for w in range(owners):
-
-                @pl.when(member != w)
-                def _():
-                    near_copy(layer, w, member).wait_send()
-                    near_copy(layer, w, w).wait_recv()
-
-            for i in range(2):
-                term = near[0, i].astype(F32)
-                for w in range(1, owners):
-                    term = term + near[w, i].astype(F32)
-                sums_of[layer][0, i] = term.astype(near.dtype)
-
-            @pl.when(group != 0)
-            def _():
-                far_copy(layer, group).start()
 
     decoded = encodes[3]
     for layer in range(3, -1, -1):
@@ -408,29 +415,38 @@
 
     @pl.when(phase == top)
     def _():
-        wait_all(copy_cot)
-        cols_all[0] = cols_send[me]
-        wait_all(copy_cols)
-        wait_all(copy_slope)
         span = micro * heights[top]
 
-        def terms(slot):
-            cols = cols_all[slot].astype(BF16)
+        def terms(sender):
+            @pl.when(sender != me)
+            def _():
+                copy_cot(me, sender).wait_recv()
+                copy_cols(me, sender).wait_recv()
+                copy_slope(me, sender).wait_recv()
+
+            cols = cols_all[sender].astype(BF16)
             return (
-                dot(cols[:, :span], slope_all[slot]),
-                dot(cols[:, span:], cot_all[slot]),
+                dot(cols[:, :span], slope_all[sender]),
+                dot(cols[:, span:], cot_all[sender]),
             )
 
         total = terms(0)
         if replicas <= 16:
-            for slot in range(1, replicas):
-                total = jax.tree.map(jnp.add, total, terms(slot))
+            for sender in range(1, replicas):
+                total = jax.tree.map(jnp.add, total, terms(sender))
         else:
             total = lax.fori_loop(
                 1, replicas, lambda s, t: jax.tree.map(jnp.add, t, terms(s)), total
             )
         for i in range(2):
             put_grad(top, i, total[i])
+
+        @others
+        def _(to):
+            copy_cot(to, me).wait_send()
+            copy_cols(to, me).wait_send()
+            copy_slope(to, me).wait_send()
+
 
     for q in range(grad_out.shape[2] // LANES):
         grad_out[0, :, q * LANES : (q + 1) * LANES] = pack_g[2 * q : 2 * q + 2, :]

time: 27 us -> 25.8 us (0.956)
  the two profiles are of different devices: /device:TPU:3 before, /device:TPU:2 now
where the time goes in v2:
time: 25.8 us; the launch traced here: 25.6 us
  Pallas kernels  25 us (97%)
  between operations  0.65 us (3%)
    pallas_call x1, Pallas kernels, on_device(): pl.pallas_call(functools.partial(kernel, replicas, heights, widths, micro...  24.2 us
    pallas_call x1, Pallas kernels, on_device(): pl.pallas_call(deliver, out_shape=(jax.ShapeDtypeStruct((1, micro, elemen...  0.73 us

profile of v2, /device:TPU:2, one launch (start us, length us, event | category | flops | bytes accessed | tf_op | source)
XLA Modules:
  0.0 25.6 jit_solution(1469936175017880877)
XLA Ops:
  0.6 24.2 %shard_map.275 = (bf16[1,2,16384]{2,1,0:T(2,128)(2,1)S(1)}, f32[1,2,32768]{2,1,0:T(2,128)S(1)}) custom-call(bf16[2,16384]{1,0:T(2,128)(2,1)} %refs_0_.1, s32[1,2]{1,0:T(1,128)} %bitcast.11, s32[27,2,256]{2,1,0:T(2,128)} %bitcast.6, s32[27,2,128]{2,1,0:T(2,128)} %bitcast.7, s32[27,2,64]{2,1,0:T(2,128)} %bitcast.8, s32[27,2,32]{2,1,0:T(2,128)} %bitcast.9, ...), custom_call_target="tpu_custom_call" | custom-call | tf_op jit(solution)/shard_map/pallas_call | solution.py:515
  24.9 0.7 %shard_map.276 = (bf16[1,2,16384]{2,1,0:T(2,128)(2,1)}, f32[1,2,32768]{2,1,0:T(2,128)}) custom-call(bf16[1,2,16384]{2,1,0:T(2,128)(2,1)S(1)} %get-tuple-element.4.dec_in, f32[1,2,32768]{2,1,0:T(2,128)S(1)} %get-tuple-element.5.grad_in), custom_call_target="tpu_custom_call" | custom-call | tf_op jit(solution)/shard_map/pallas_call | solution.py:528

commit v3 on v2

--- a/solution.py
+++ b/solution.py
@@ -80,6 +80,15 @@
         recv_cols,
         send_near,
         recv_near,
+        aim_mid,
+        got_help,
+        send_aim,
+        recv_aim,
+        send_mid,
+        recv_mid,
+        send_far,
+        recv_far,
+        recv_help,
     ) = refs
     nears, sums_of = (near0, near1, near2), (sum0, sum1, sum2)
     features, counts, cot = held[0], held[1], held[27]
@@ -101,11 +110,30 @@
     for i in order + [26, 25, 24]:
         load(i).start()
 
+    mid, helper = 2, 0
     barrier = pltpu.get_barrier_semaphore()
 
     @pl.loop(1, replicas)
     def _(offset):
         pl.semaphore_signal(barrier, inc=1, device_id=peer(offset), device_id_type=MESH)
+
+    mid_owners = part2.shape[0]
+    mid_groups = replicas // mid_owners
+
+    @pl.when(phase == helper)
+    def _():
+        pl.semaphore_signal(barrier, inc=1, device_id={"phase": mid, "dp": me}, device_id_type=MESH)
+
+    @pl.when((phase == mid) & (me < mid_owners))
+    def _():
+        @pl.loop(0, mid_groups)
+        def _(group):
+            pl.semaphore_signal(
+                barrier,
+                inc=1,
+                device_id={"phase": helper, "dp": group * mid_owners + me},
+                device_id_type=MESH,
+            )
 
     for i in (0, 27):
         load(i).wait()
@@ -184,6 +212,76 @@
     @pl.when(phase == top)
     def _():
         cot_all[me] = target(top)
+
+    @pl.when(phase == mid)
+    def _():
+        aim_mid[0] = target(mid)
+
+    aim_copy = pltpu.make_async_remote_copy(
+        src_ref=aim_mid.at[0],
+        dst_ref=aim_mid.at[1],
+        send_sem=send_aim.at[0],
+        recv_sem=recv_aim.at[0],
+        device_id={"phase": helper, "dp": me},
+        device_id_type=MESH,
+    )
+
+    def mid_near(w, sender):
+        _, group, _ = group_of(mid)
+        return pltpu.make_async_remote_copy(
+            src_ref=part2.at[w],
+            dst_ref=near2.at[sender],
+            send_sem=send_mid.at[w],
+            recv_sem=recv_mid.at[sender],
+            device_id={"phase": phase, "dp": group * mid_owners + w},
+            device_id_type=MESH,
+        )
+
+    def mid_far(got, recv_sem, group):
+        return pltpu.make_async_remote_copy(
+            src_ref=sum2.at[0],
+            dst_ref=got.at[group],
+            send_sem=send_far.at[0],
+            recv_sem=recv_sem.at[group],
+            device_id={"phase": mid, "dp": group_of(mid)[2]},
+            device_id_type=MESH,
+        )
+
+    def mid_start(term):
+        rows_here = part2.shape[1]
+        member = group_of(mid)[2]
+        for w in range(mid_owners):
+            part2[w] = term[w * rows_here : (w + 1) * rows_here].astype(part2.dtype)
+        for w in range(mid_owners):
+
+            @pl.when(member != w)
+            def _():
+                mid_near(w, member).start()
+
+    def mid_pass():
+        @pl.when((phase == mid) | (phase == helper))
+        def _():
+            _, group, member = group_of(mid)
+            near2[member] = part2[member]
+            for w in range(mid_owners):
+
+                @pl.when(member != w)
+                def _():
+                    mid_near(w, member).wait_send()
+                    mid_near(w, w).wait_recv()
+
+            term = near2[0].astype(F32)
+            for w in range(1, mid_owners):
+                term = term + near2[w].astype(F32)
+            sum2[0] = term.astype(near2.dtype)
+
+            @pl.when(phase == helper)
+            def _():
+                mid_far(got_help, recv_help, group).start()
+
+            @pl.when((phase == mid) & (group != 0))
+            def _():
+                mid_far(got2, recv_far, group).start()
 
     for i in (2, 3, 4, 5, 6, 7, 8, 1):
         load(i).wait()
@@ -276,7 +374,19 @@
         encoded = (x.astype(F32) + dot(active, sws[layer][...])).astype(BF16)
         encodes.append(encoded)
         if layer == 0:
-            pl.semaphore_wait(barrier, replicas - 1)
+            paired = (phase == helper) | (phase == mid)
+
+            @pl.when(paired)
+            def _():
+                pl.semaphore_wait(barrier, replicas)
+
+            @pl.when(jnp.logical_not(paired))
+            def _():
+                pl.semaphore_wait(barrier, replicas - 1)
+
+            @pl.when(phase == mid)
+            def _():
+                aim_copy.start()
 
             @pl.when(phase == top)
             def _():
@@ -284,7 +394,7 @@
 
         @pl.when(phase == layer)
         def _():
-            aim = target(layer) if layer < top else cot_all[me]
+            aim = target(layer) if layer < mid else (aim_mid[0] if layer == mid else cot_all[me])
             backward = dot_nt(aim, sws[layer][...])
             grad = 0.5 * (1.0 + bend) + 0.5 * inner * (1.0 - bend * bend) * GELU_A * (
                 1.0 + 3.0 * GELU_B * squared
@@ -305,6 +415,8 @@
                     copy_cols(to, me).start()
                     copy_slope(to, me).start()
 
+            elif layer == mid:
+                mid_start(dot_tn(normed, slope))
             else:
                 part = parts[layer]
                 owners, _, rows_here, _ = part.shape
@@ -317,7 +429,16 @@
                     def _():
                         near_copy(layer, w, group_of(layer)[2]).start()
 
-        if layer > 0:
+        if layer == mid:
+
+            @pl.when(phase == helper)
+            def _():
+                aim_copy.wait_recv()
+                mid_start(dot_tn(active, aim_mid[1]))
+
+        if layer == top:
+            mid_pass()
+        elif layer > 0:
             pass_on(layer - 1)
 
         if layer < 3:
@@ -390,7 +511,31 @@
                     :, h * LANES : (h + 1) * LANES
                 ]
 
-    for layer in range(3):
+    @pl.when(phase == helper)
+    def _():
+        mid_far(got_help, recv_help, 0).wait_send()
+
+    @pl.when(phase == mid)
+    def _():
+        aim_copy.wait_send()
+        group = group_of(mid)[1]
+
+        @pl.when(group != 0)
+        def _():
+            mid_far(got2, recv_far, 0).wait_send()
+
+        @pl.when(group == 0)
+        def _():
+            got2[0] = sum2[0]
+            for i, (got, recv_sem) in enumerate(((got2, recv_far), (got_help, recv_help))):
+                for sender in range(1 - i, mid_groups):
+                    mid_far(got, recv_sem, sender).wait_recv()
+                term = got[0].astype(F32)
+                for sender in range(1, mid_groups):
+                    term = term + got[sender].astype(F32)
+                put_grad(mid, i, term)
+
+    for layer in range(2):
         got = gots[layer]
 
         @pl.when(phase == layer)
@@ -483,6 +628,11 @@
         rows_here = min(widths[layer], owned // widths[layer])
         owners = widths[layer] // rows_here
         kind = narrow(rows_here)
+        if layer == 2:
+            shape = (rows_here, widths[2])
+            for held, first in ((parts, owners), (gots, replicas // owners), (nears, owners), (sums_of, 1)):
+                held.append(pltpu.VMEM((first, *shape), kind))
+            break
         parts.append(pltpu.VMEM((owners, 2, rows_here, widths[layer]), kind))
         gots.append(pltpu.VMEM((replicas // owners, 2, rows_here, widths[layer]), kind))
         nears.append(pltpu.VMEM((owners, 2, rows_here, widths[layer]), kind))
@@ -511,6 +661,9 @@
         pltpu.VMEM((replicas, top_rows, 2 * span), narrow(top_rows)),
         pltpu.VMEM((replicas, top_rows, 2 * span), narrow(top_rows)),
         *[sem] * 10,
+        pltpu.VMEM((2, micro * heights[2], widths[2]), BF16),
+        gots[2],
+        *[sem] * 7,
     ]
     held = pl.pallas_call(
         functools.partial(kernel, replicas, heights, widths, micro, len(arrays)),

time: 25.8 us -> 24.3 us (0.942)
  the two profiles are of different devices: /device:TPU:2 before, /device:TPU:11 now
where the time goes in v3:
time: 24.3 us; the launch traced here: 24.2 us
  Pallas kernels  23.5 us (97%)
  between operations  0.65 us (3%)
    pallas_call x1, Pallas kernels, on_device(): pl.pallas_call(functools.partial(kernel, replicas, heights, widths, micro...  22.8 us
    pallas_call x1, Pallas kernels, on_device(): pl.pallas_call(deliver, out_shape=(jax.ShapeDtypeStruct((1, micro, elemen...  0.73 us

profile of v3, /device:TPU:11, one launch (start us, length us, event | category | flops | bytes accessed | tf_op | source)
XLA Modules:
  0.0 24.2 jit_solution(12334104406622969893)
XLA Ops:
  0.6 22.8 %shard_map.275 = (bf16[1,2,16384]{2,1,0:T(2,128)(2,1)S(1)}, f32[1,2,32768]{2,1,0:T(2,128)S(1)}) custom-call(bf16[2,16384]{1,0:T(2,128)(2,1)} %refs_0_.1, s32[1,2]{1,0:T(1,128)} %bitcast.11, s32[27,2,256]{2,1,0:T(2,128)} %bitcast.6, s32[27,2,128]{2,1,0:T(2,128)} %bitcast.7, s32[27,2,64]{2,1,0:T(2,128)} %bitcast.8, s32[27,2,32]{2,1,0:T(2,128)} %bitcast.9, ...), custom_call_target="tpu_custom_call" | custom-call | tf_op jit(solution)/shard_map/pallas_call | solution.py:668
  23.4 0.7 %shard_map.276 = (bf16[1,2,16384]{2,1,0:T(2,128)(2,1)}, f32[1,2,32768]{2,1,0:T(2,128)}) custom-call(bf16[1,2,16384]{2,1,0:T(2,128)(2,1)S(1)} %get-tuple-element.4.dec_in, f32[1,2,32768]{2,1,0:T(2,128)S(1)} %get-tuple-element.5.grad_in), custom_call_target="tpu_custom_call" | custom-call | tf_op jit(solution)/shard_map/pallas_call | solution.py:681

commit v4 on v3

--- a/solution.py
+++ b/solution.py
@@ -89,6 +89,8 @@
         send_far,
         recv_far,
         recv_help,
+        relay_cot,
+        relay_slope,
     ) = refs
     nears, sums_of = (near0, near1, near2), (sum0, sum1, sum2)
     features, counts, cot = held[0], held[1], held[27]
@@ -161,7 +163,7 @@
     top = 3
 
     def all_send(source, gathered, send_sem, recv_sem, indexed):
-        def copy(to, sender):
+        def copy(to, sender, send_sem=send_sem):
             return pltpu.make_async_remote_copy(
                 src_ref=source.at[to] if indexed else source.at[sender],
                 dst_ref=gathered.at[sender],
@@ -177,12 +179,31 @@
     copy_slope = all_send(slope_all, slope_all, send_slope, recv_slope, False)
     copy_cols = all_send(cols_send, cols_all, send_cols, recv_cols, True)
 
+    partner = me + 1 - 2 * lax.rem(me, 2)
+
+    def alike(other):
+        return lax.rem(other, 2) == lax.rem(me, 2)
+
     def others(body):
         @pl.loop(0, replicas)
         def _(other):
             @pl.when(other != me)
             def _():
                 body(other)
+
+    def direct(body):
+        @others
+        def _(to):
+            @pl.when(alike(to) | (to == partner))
+            def _():
+                body(to)
+
+    def column(body):
+        @others
+        def _(sender):
+            @pl.when(alike(sender))
+            def _():
+                body(sender)
 
     def group_of(layer):
         owners = parts[layer].shape[0]
@@ -390,7 +411,7 @@
 
             @pl.when(phase == top)
             def _():
-                others(lambda to: copy_cot(to, me).start())
+                direct(lambda to: copy_cot(to, me).start())
 
         @pl.when(phase == layer)
         def _():
@@ -413,6 +434,9 @@
                 @others
                 def _(to):
                     copy_cols(to, me).start()
+
+                @direct
+                def _(to):
                     copy_slope(to, me).start()
 
             elif layer == mid:
@@ -562,11 +586,25 @@
     def _():
         span = micro * heights[top]
 
+        @column
+        def _(sender):
+            copy_cot(me, sender).wait_recv()
+            copy_cot(partner, sender, relay_cot).start()
+
+        def relay(sender):
+            @pl.when(alike(sender) & (sender != me))
+            def _():
+                copy_slope(me, sender).wait_recv()
+                copy_slope(partner, sender, relay_slope).start()
+
         def terms(sender):
             @pl.when(sender != me)
             def _():
+                copy_cols(me, sender).wait_recv()
+
+            @pl.when(jnp.logical_not(alike(sender)))
+            def _():
                 copy_cot(me, sender).wait_recv()
-                copy_cols(me, sender).wait_recv()
                 copy_slope(me, sender).wait_recv()
 
             cols = cols_all[sender].astype(BF16)
@@ -575,22 +613,36 @@
                 dot(cols[:, span:], cot_all[sender]),
             )
 
-        total = terms(0)
         if replicas <= 16:
-            for sender in range(1, replicas):
-                total = jax.tree.map(jnp.add, total, terms(sender))
+            relay(0)
+            relay(1)
+            total = None
+            for sender in range(replicas):
+                if sender + 2 < replicas:
+                    relay(sender + 2)
+                new = terms(sender)
+                total = new if total is None else jax.tree.map(jnp.add, total, new)
         else:
+            pl.loop(0, replicas)(relay)
             total = lax.fori_loop(
-                1, replicas, lambda s, t: jax.tree.map(jnp.add, t, terms(s)), total
+                1, replicas, lambda s, t: jax.tree.map(jnp.add, t, terms(s)), terms(0)
             )
         for i in range(2):
             put_grad(top, i, total[i])
 
         @others
         def _(to):
+            copy_cols(to, me).wait_send()
+
+        @direct
+        def _(to):
             copy_cot(to, me).wait_send()
-            copy_cols(to, me).wait_send()
             copy_slope(to, me).wait_send()
+
+        @column
+        def _(sender):
+            copy_cot(partner, sender, relay_cot).wait_send()
+            copy_slope(partner, sender, relay_slope).wait_send()
 
 
     for q in range(grad_out.shape[2] // LANES):
@@ -663,7 +715,7 @@
         *[sem] * 10,
         pltpu.VMEM((2, micro * heights[2], widths[2]), BF16),
         gots[2],
-        *[sem] * 7,
+        *[sem] * 9,
     ]
     held = pl.pallas_call(
         functools.partial(kernel, replicas, heights, widths, micro, len(arrays)),

time: 24.3 us -> 25.7 us (1.058)
  the two profiles are of different devices: /device:TPU:11 before, /device:TPU:3 now
where the time goes in v4:
time: 25.7 us; the launch traced here: 25.2 us
  Pallas kernels  24.6 us (96%)
  between operations  0.65 us (3%)
    pallas_call x1, Pallas kernels, on_device(): pl.pallas_call(functools.partial(kernel, replicas, heights, widths, micro...  23.8 us
    pallas_call x1, Pallas kernels, on_device(): pl.pallas_call(deliver, out_shape=(jax.ShapeDtypeStruct((1, micro, elemen...  0.73 us

profile of v4, /device:TPU:3, one launch (start us, length us, event | category | flops | bytes accessed | tf_op | source)
XLA Modules:
  0.0 25.2 jit_solution(5056826097935470045)
XLA Ops:
  0.6 23.8 %shard_map.275 = (bf16[1,2,16384]{2,1,0:T(2,128)(2,1)S(1)}, f32[1,2,32768]{2,1,0:T(2,128)S(1)}) custom-call(bf16[2,16384]{1,0:T(2,128)(2,1)} %refs_0_.1, s32[1,2]{1,0:T(1,128)} %bitcast.11, s32[27,2,256]{2,1,0:T(2,128)} %bitcast.6, s32[27,2,128]{2,1,0:T(2,128)} %bitcast.7, s32[27,2,64]{2,1,0:T(2,128)} %bitcast.8, s32[27,2,32]{2,1,0:T(2,128)} %bitcast.9, ...), custom_call_target="tpu_custom_call" | custom-call | tf_op jit(solution)/shard_map/pallas_call | solution.py:720
  24.5 0.7 %shard_map.276 = (bf16[1,2,16384]{2,1,0:T(2,128)(2,1)}, f32[1,2,32768]{2,1,0:T(2,128)}) custom-call(bf16[1,2,16384]{2,1,0:T(2,128)(2,1)S(1)} %get-tuple-element.4.dec_in, f32[1,2,32768]{2,1,0:T(2,128)S(1)} %get-tuple-element.5.grad_in), custom_call_target="tpu_custom_call" | custom-call | tf_op jit(solution)/shard_map/pallas_call | solution.py:733

commit v5 on v3

--- a/solution.py
+++ b/solution.py
@@ -66,18 +66,8 @@
         sum0,
         sum1,
         sum2,
-        cot_all,
-        slope_all,
-        cols_send,
-        cols_all,
         send_part,
         recv_part,
-        send_cot,
-        recv_cot,
-        send_slope,
-        recv_slope,
-        send_cols,
-        recv_cols,
         send_near,
         recv_near,
         aim_mid,
@@ -89,6 +79,21 @@
         send_far,
         recv_far,
         recv_help,
+        aim_top,
+        pair_l,
+        pair_r,
+        held_sum,
+        blocks,
+        got_first,
+        got_second,
+        send_top,
+        send_l,
+        recv_l,
+        send_r,
+        recv_r,
+        send_block,
+        recv_first,
+        recv_second,
     ) = refs
     nears, sums_of = (near0, near1, near2), (sum0, sum1, sum2)
     features, counts, cot = held[0], held[1], held[27]
@@ -110,7 +115,10 @@
     for i in order + [26, 25, 24]:
         load(i).start()
 
-    mid, helper = 2, 0
+    mid, helper, aid = 2, 0, 1
+    half = replicas // 2
+    partner = me + 1 - 2 * lax.rem(me, 2)
+    odd = lax.rem(me, 2)
     barrier = pltpu.get_barrier_semaphore()
 
     @pl.loop(1, replicas)
@@ -133,6 +141,19 @@
                 inc=1,
                 device_id={"phase": helper, "dp": group * mid_owners + me},
                 device_id_type=MESH,
+            )
+
+    @pl.when(phase == aid)
+    def _():
+        for to in (me, partner):
+            pl.semaphore_signal(barrier, inc=1, device_id={"phase": 3, "dp": to}, device_id_type=MESH)
+
+    @pl.when(phase == 3)
+    def _():
+        @pl.loop(0, half)
+        def _(w):
+            pl.semaphore_signal(
+                barrier, inc=1, device_id={"phase": aid, "dp": 2 * w + odd}, device_id_type=MESH
             )
 
     for i in (0, 27):
@@ -160,29 +181,59 @@
 
     top = 3
 
-    def all_send(source, gathered, send_sem, recv_sem, indexed):
-        def copy(to, sender):
-            return pltpu.make_async_remote_copy(
-                src_ref=source.at[to] if indexed else source.at[sender],
-                dst_ref=gathered.at[sender],
-                send_sem=send_sem.at[to],
-                recv_sem=recv_sem.at[sender],
-                device_id={"phase": phase, "dp": to},
-                device_id_type=MESH,
+    def aim_send(slot):
+        return pltpu.make_async_remote_copy(
+            src_ref=aim_top.at[0],
+            dst_ref=pair_r.at[slot],
+            send_sem=send_top.at[slot],
+            recv_sem=recv_r.at[slot],
+            device_id={"phase": aid, "dp": partner if slot else me},
+            device_id_type=MESH,
+        )
+
+    def swap(pair, send_sem, recv_sem):
+        return pltpu.make_async_remote_copy(
+            src_ref=pair.at[0],
+            dst_ref=pair.at[1],
+            send_sem=send_sem.at[0],
+            recv_sem=recv_sem.at[1],
+            device_id={"phase": phase, "dp": partner},
+            device_id_type=MESH,
+        )
+
+    swap_l, swap_r = swap(pair_l, send_l, recv_l), swap(pair_r, send_r, recv_r)
+
+    def block_copy(got, recv_sem, w, sender):
+        return pltpu.make_async_remote_copy(
+            src_ref=blocks.at[w],
+            dst_ref=got.at[sender],
+            send_sem=send_block.at[w],
+            recv_sem=recv_sem.at[sender],
+            device_id={"phase": top, "dp": 2 * w + odd},
+            device_id_type=MESH,
+        )
+
+    def outer(slot):
+        turned = pair_l[slot].astype(F32).T
+        rows_here = blocks.shape[1]
+        picked = [
+            jnp.where(
+                odd == 0,
+                turned[2 * w * rows_here : (2 * w + 1) * rows_here],
+                turned[(2 * w + 1) * rows_here : (2 * w + 2) * rows_here],
             )
-
-        return copy
-
-    copy_cot = all_send(cot_all, cot_all, send_cot, recv_cot, False)
-    copy_slope = all_send(slope_all, slope_all, send_slope, recv_slope, False)
-    copy_cols = all_send(cols_send, cols_all, send_cols, recv_cols, True)
-
-    def others(body):
-        @pl.loop(0, replicas)
-        def _(other):
-            @pl.when(other != me)
-            def _():
-                body(other)
+            for w in range(half)
+        ]
+        return dot(jnp.concatenate(picked, axis=0).astype(BF16), pair_r[slot])
+
+    def pair_first():
+        held_sum[...] = outer(0)
+
+    def pair_second():
+        rows_here = blocks.shape[1]
+        total = held_sum[...] + outer(1)
+        for w in range(half):
+            blocks[w] = total[w * rows_here : (w + 1) * rows_here].astype(blocks.dtype)
 
     def group_of(layer):
         owners = parts[layer].shape[0]
@@ -211,7 +262,7 @@
 
     @pl.when(phase == top)
     def _():
-        cot_all[me] = target(top)
+        aim_top[0] = target(top)
 
     @pl.when(phase == mid)
     def _():
@@ -367,22 +418,39 @@
         mixed = mixes[0] if len(mixes) == 1 else jnp.concatenate(mixes, axis=0)
         normed_f = mixed * lax.rsqrt(jnp.mean(mixed * mixed, axis=1, keepdims=True) + 1e-05)
         normed = normed_f.astype(BF16)
+        if layer == top:
+
+            @pl.when(phase == top)
+            def _():
+                pair_l[0] = normed
+                swap_l.start()
+
         inner = dot(normed, fws[layer][...])
         squared = inner * inner
         bend = jnp.tanh(GELU_A * inner * (1.0 + GELU_B * squared))
         active = (0.5 * inner * (1.0 + bend)).astype(BF16)
+        if layer == top:
+
+            @pl.when(phase == aid)
+            def _():
+                pair_l[0] = active
+                swap_l.start()
+                aim_send(0).wait_recv()
+                pair_first()
+
         encoded = (x.astype(F32) + dot(active, sws[layer][...])).astype(BF16)
         encodes.append(encoded)
         if layer == 0:
-            paired = (phase == helper) | (phase == mid)
-
-            @pl.when(paired)
-            def _():
-                pl.semaphore_wait(barrier, replicas)
-
-            @pl.when(jnp.logical_not(paired))
-            def _():
-                pl.semaphore_wait(barrier, replicas - 1)
+            for which, count in (
+                (helper, replicas),
+                (mid, replicas),
+                (aid, replicas - 1 + half),
+                (top, replicas + 1),
+            ):
+
+                @pl.when(phase == which)
+                def _():
+                    pl.semaphore_wait(barrier, count)
 
             @pl.when(phase == mid)
             def _():
@@ -390,31 +458,21 @@
 
             @pl.when(phase == top)
             def _():
-                others(lambda to: copy_cot(to, me).start())
+                aim_send(0).start()
+                aim_send(1).start()
 
         @pl.when(phase == layer)
         def _():
-            aim = target(layer) if layer < mid else (aim_mid[0] if layer == mid else cot_all[me])
+            aim = target(layer) if layer < mid else (aim_mid[0] if layer == mid else aim_top[0])
             backward = dot_nt(aim, sws[layer][...])
             grad = 0.5 * (1.0 + bend) + 0.5 * inner * (1.0 - bend * bend) * GELU_A * (
                 1.0 + 3.0 * GELU_B * squared
             )
             slope = (grad * backward).astype(BF16)
             if layer == top:
-                slope_all[me] = slope
-                both = jnp.concatenate(
-                    [normed.astype(F32).T, active.astype(F32).T], axis=1
-                ).astype(cols_send.dtype)
-                rows_here = cols_send.shape[1]
-                for d in range(replicas):
-                    cols_send[d] = both[d * rows_here : (d + 1) * rows_here]
-                cols_all[me] = cols_send[me]
-
-                @others
-                def _(to):
-                    copy_cols(to, me).start()
-                    copy_slope(to, me).start()
-
+                pair_r[0] = slope
+                swap_r.start()
+                pair_first()
             elif layer == mid:
                 mid_start(dot_tn(normed, slope))
             else:
@@ -487,6 +545,24 @@
                             :, h * LANES : (h + 1) * LANES
                         ]
 
+    rank = lax.div(me, 2)
+
+    @pl.when((phase == top) | (phase == aid))
+    def _():
+        swap_l.wait_recv()
+        swap_r.wait_recv()
+        pair_second()
+
+        @pl.loop(0, half)
+        def _(w):
+            @pl.when(phase == aid)
+            def _():
+                block_copy(got_second, recv_second, w, rank).start()
+
+            @pl.when((phase == top) & (w != rank))
+            def _():
+                block_copy(got_first, recv_first, w, rank).start()
+
     for j in range(chunks):
         dec_out[0, :, j * LANES : (j + 1) * LANES] = pack_d[2 * j : 2 * j + 2, :].astype(BF16)
 
@@ -558,40 +634,43 @@
                         term = term + got[sender, i].astype(F32)
                     put_grad(layer, i, term)
 
+    @pl.when(phase == aid)
+    def _():
+        swap_l.wait_send()
+
+        @pl.loop(0, half)
+        def _(w):
+            block_copy(got_second, recv_second, w, rank).wait_send()
+
     @pl.when(phase == top)
     def _():
-        span = micro * heights[top]
-
-        def terms(sender):
-            @pl.when(sender != me)
-            def _():
-                copy_cot(me, sender).wait_recv()
-                copy_cols(me, sender).wait_recv()
-                copy_slope(me, sender).wait_recv()
-
-            cols = cols_all[sender].astype(BF16)
-            return (
-                dot(cols[:, :span], slope_all[sender]),
-                dot(cols[:, span:], cot_all[sender]),
-            )
-
-        total = terms(0)
-        if replicas <= 16:
-            for sender in range(1, replicas):
-                total = jax.tree.map(jnp.add, total, terms(sender))
-        else:
-            total = lax.fori_loop(
-                1, replicas, lambda s, t: jax.tree.map(jnp.add, t, terms(s)), total
-            )
-        for i in range(2):
-            put_grad(top, i, total[i])
-
-        @others
-        def _(to):
-            copy_cot(to, me).wait_send()
-            copy_cols(to, me).wait_send()
-            copy_slope(to, me).wait_send()
-
+        swap_l.wait_send()
+        swap_r.wait_send()
+        aim_send(0).wait_send()
+        aim_send(1).wait_send()
+        got_first[rank] = blocks[rank]
+
+        def received(got, recv_sem, sender, own):
+            @pl.when((sender != rank) | (not own))
+            def _():
+                block_copy(got, recv_sem, 0, sender).wait_recv()
+
+            return got[sender].astype(F32)
+
+        for i, (got, recv_sem) in enumerate(((got_second, recv_second), (got_first, recv_first))):
+            first = functools.partial(received, got, recv_sem, own=i == 1)
+            total = lax.fori_loop(1, half, lambda w, t: t + first(w), first(0)) if half > 8 else None
+            if total is None:
+                total = first(0)
+                for w in range(1, half):
+                    total = total + first(w)
+            put_grad(top, 1 - i, total)
+
+        @pl.loop(0, half)
+        def _(w):
+            @pl.when(w != rank)
+            def _():
+                block_copy(got_first, recv_first, w, rank).wait_send()
 
     for q in range(grad_out.shape[2] // LANES):
         grad_out[0, :, q * LANES : (q + 1) * LANES] = pack_g[2 * q : 2 * q + 2, :]
@@ -656,14 +735,16 @@
         *gots,
         *nears,
         *sums_of,
-        pltpu.VMEM((replicas, span, widths[3]), BF16),
-        pltpu.VMEM((replicas, span, widths[3]), BF16),
-        pltpu.VMEM((replicas, top_rows, 2 * span), narrow(top_rows)),
-        pltpu.VMEM((replicas, top_rows, 2 * span), narrow(top_rows)),
-        *[sem] * 10,
+        *[sem] * 4,
         pltpu.VMEM((2, micro * heights[2], widths[2]), BF16),
         gots[2],
         *[sem] * 7,
+        pltpu.VMEM((1, span, widths[3]), BF16),
+        pltpu.VMEM((2, span, widths[3]), BF16),
+        pltpu.VMEM((2, span, widths[3]), BF16),
+        pltpu.VMEM((replicas // 2 * top_rows, widths[3]), F32),
+        *[pltpu.VMEM((replicas // 2, top_rows, widths[3]), narrow(top_rows))] * 3,
+        *[sem] * 8,
     ]
     held = pl.pallas_call(
         functools.partial(kernel, replicas, heights, widths, micro, len(arrays)),

time: 24.3 us -> 25.1 us (1.033)
  the two profiles are of different devices: /device:TPU:11 before, /device:TPU:3 now
where the time goes in v5:
time: 25.1 us; the launch traced here: 24.7 us
  Pallas kernels  24 us (96%)
  between operations  0.65 us (3%)
    pallas_call x1, Pallas kernels, on_device(): pl.pallas_call(functools.partial(kernel, replicas, heights, widths, micro...  23.3 us
    pallas_call x1, Pallas kernels, on_device(): pl.pallas_call(deliver, out_shape=(jax.ShapeDtypeStruct((1, micro, elemen...  0.73 us

profile of v5, /device:TPU:3, one launch (start us, length us, event | category | flops | bytes accessed | tf_op | source)
XLA Modules:
  0.0 24.7 jit_solution(14517971135171151425)
XLA Ops:
  0.6 23.3 %shard_map.275 = (bf16[1,2,16384]{2,1,0:T(2,128)(2,1)S(1)}, f32[1,2,32768]{2,1,0:T(2,128)S(1)}) custom-call(bf16[2,16384]{1,0:T(2,128)(2,1)} %refs_0_.1, s32[1,2]{1,0:T(1,128)} %bitcast.11, s32[27,2,256]{2,1,0:T(2,128)} %bitcast.6, s32[27,2,128]{2,1,0:T(2,128)} %bitcast.7, s32[27,2,64]{2,1,0:T(2,128)} %bitcast.8, s32[27,2,32]{2,1,0:T(2,128)} %bitcast.9, ...), custom_call_target="tpu_custom_call" | custom-call | tf_op jit(solution)/shard_map/pallas_call | solution.py:749
  24.0 0.7 %shard_map.276 = (bf16[1,2,16384]{2,1,0:T(2,128)(2,1)}, f32[1,2,32768]{2,1,0:T(2,128)}) custom-call(bf16[1,2,16384]{2,1,0:T(2,128)(2,1)S(1)} %get-tuple-element.4.dec_in, f32[1,2,32768]{2,1,0:T(2,128)S(1)} %get-tuple-element.5.grad_in), custom_call_target="tpu_custom_call" | custom-call | tf_op jit(solution)/shard_map/pallas_call | solution.py:762

commit v6 on v2

--- a/solution.py
+++ b/solution.py
@@ -62,10 +62,8 @@
         got2,
         near0,
         near1,
-        near2,
         sum0,
         sum1,
-        sum2,
         cot_all,
         slope_all,
         cols_send,
@@ -80,8 +78,20 @@
         recv_cols,
         send_near,
         recv_near,
+        aim_mid,
+        got_help,
+        send_aim,
+        recv_aim,
+        send_mid,
+        recv_mid,
+        recv_help,
+        aim_top,
+        send_top,
+        recv_top,
+        send_front,
+        recv_front,
     ) = refs
-    nears, sums_of = (near0, near1, near2), (sum0, sum1, sum2)
+    nears, sums_of = (near0, near1), (sum0, sum1)
     features, counts, cot = held[0], held[1], held[27]
     kms, pms, dws = held[2:6], held[6:9], held[9:13]
     fws, sws = held[13:17], held[17:21]
@@ -101,11 +111,42 @@
     for i in order + [26, 25, 24]:
         load(i).start()
 
+    mid, helper, aid = 2, 0, 1
+    cut = cot_all.shape[1] // 2
     barrier = pltpu.get_barrier_semaphore()
 
     @pl.loop(1, replicas)
     def _(offset):
         pl.semaphore_signal(barrier, inc=1, device_id=peer(offset), device_id_type=MESH)
+
+    mid_owners = part2.shape[0]
+
+    @pl.when(phase == helper)
+    def _():
+        pl.semaphore_signal(barrier, inc=1, device_id={"phase": mid, "dp": me}, device_id_type=MESH)
+
+    @pl.when((phase == mid) & (me < mid_owners))
+    def _():
+        @pl.loop(0, replicas)
+        def _(to):
+            pl.semaphore_signal(
+                barrier, inc=1, device_id={"phase": helper, "dp": to}, device_id_type=MESH
+            )
+
+    @pl.when(phase == aid)
+    def _():
+        pl.semaphore_signal(barrier, inc=1, device_id={"phase": 3, "dp": me}, device_id_type=MESH)
+
+    @pl.when(phase == 3)
+    def _():
+        @pl.loop(1, replicas)
+        def _(offset):
+            pl.semaphore_signal(
+                barrier,
+                inc=1,
+                device_id={"phase": aid, "dp": lax.rem(me + offset, replicas)},
+                device_id_type=MESH,
+            )
 
     for i in (0, 27):
         load(i).wait()
@@ -132,22 +173,38 @@
 
     top = 3
 
-    def all_send(source, gathered, send_sem, recv_sem, indexed):
-        def copy(to, sender):
-            return pltpu.make_async_remote_copy(
-                src_ref=source.at[to] if indexed else source.at[sender],
-                dst_ref=gathered.at[sender],
-                send_sem=send_sem.at[to],
-                recv_sem=recv_sem.at[sender],
-                device_id={"phase": phase, "dp": to},
-                device_id_type=MESH,
-            )
-
-        return copy
-
-    copy_cot = all_send(cot_all, cot_all, send_cot, recv_cot, False)
-    copy_slope = all_send(slope_all, slope_all, send_slope, recv_slope, False)
-    copy_cols = all_send(cols_send, cols_all, send_cols, recv_cols, True)
+    def top_copy(source, landing, send_sem, recv_sem, to, sender):
+        return pltpu.make_async_remote_copy(
+            src_ref=source,
+            dst_ref=landing,
+            send_sem=send_sem.at[to],
+            recv_sem=recv_sem.at[sender],
+            device_id={"phase": top, "dp": to},
+            device_id_type=MESH,
+        )
+
+    def copy_cot(to, sender):
+        return top_copy(cot_all.at[sender], cot_all.at[sender], send_cot, recv_cot, to, sender)
+
+    def copy_cols(to, sender):
+        return top_copy(cols_send.at[to], cols_all.at[sender], send_cols, recv_cols, to, sender)
+
+    def copy_front(to, sender):
+        rows = slope_all.at[sender, pl.ds(0, cut)]
+        return top_copy(rows, rows, send_front, recv_front, to, sender)
+
+    def copy_back(to, sender):
+        rows = slope_all.at[sender, pl.ds(cut, cut)]
+        return top_copy(rows, rows, send_slope, recv_slope, to, sender)
+
+    top_aim = pltpu.make_async_remote_copy(
+        src_ref=cot_all.at[me],
+        dst_ref=aim_top.at[0],
+        send_sem=send_top.at[0],
+        recv_sem=recv_top.at[0],
+        device_id={"phase": aid, "dp": me},
+        device_id_type=MESH,
+    )
 
     def others(body):
         @pl.loop(0, replicas)
@@ -184,6 +241,51 @@
     @pl.when(phase == top)
     def _():
         cot_all[me] = target(top)
+
+    @pl.when(phase == mid)
+    def _():
+        aim_mid[0] = target(mid)
+
+    aim_copy = pltpu.make_async_remote_copy(
+        src_ref=aim_mid.at[0],
+        dst_ref=aim_mid.at[1],
+        send_sem=send_aim.at[0],
+        recv_sem=recv_aim.at[0],
+        device_id={"phase": helper, "dp": me},
+        device_id_type=MESH,
+    )
+
+    def mid_copy(got, recv_sem, w, sender):
+        return pltpu.make_async_remote_copy(
+            src_ref=part2.at[w],
+            dst_ref=got.at[sender],
+            send_sem=send_mid.at[w],
+            recv_sem=recv_sem.at[sender],
+            device_id={"phase": mid, "dp": w},
+            device_id_type=MESH,
+        )
+
+    def mid_start(term, helping):
+        rows_here = part2.shape[1]
+        for w in range(mid_owners):
+            part2[w] = term[w * rows_here : (w + 1) * rows_here].astype(part2.dtype)
+        mid_each(lambda copy: copy.start(), helping)
+
+    def mid_each(act, helping):
+        for w in range(mid_owners):
+            if helping:
+                act(mid_copy(got_help, recv_help, w, me))
+            else:
+
+                @pl.when(me != w)
+                def _():
+                    act(mid_copy(got2, recv_mid, w, me))
+
+    def top_cols(normed, active):
+        both = jnp.concatenate([normed.astype(F32).T, active.astype(F32).T], axis=1).astype(cols_send.dtype)
+        rows_here = cols_send.shape[1]
+        for d in range(replicas):
+            cols_send[d] = both[d * rows_here : (d + 1) * rows_here]
 
     for i in (2, 3, 4, 5, 6, 7, 8, 1):
         load(i).wait()
@@ -248,6 +350,17 @@
             def _():
                 far_copy(layer, group).start()
 
+    @pl.when(phase == top)
+    def _():
+        pl.semaphore_wait(barrier, replicas)
+        top_aim.start()
+        others(lambda to: copy_cot(to, me).start())
+
+    def bent(inner, bend, squared):
+        return 0.5 * (1.0 + bend) + 0.5 * inner * (1.0 - bend * bend) * GELU_A * (
+            1.0 + 3.0 * GELU_B * squared
+        )
+
     encodes = []
     for layer in range(4):
         for i in (9 + layer, 13 + layer, 17 + layer) + ((21 + layer,) if layer < 3 else ()):
@@ -276,35 +389,28 @@
         encoded = (x.astype(F32) + dot(active, sws[layer][...])).astype(BF16)
         encodes.append(encoded)
         if layer == 0:
-            pl.semaphore_wait(barrier, replicas - 1)
-
-            @pl.when(phase == top)
+            for which, count in ((helper, replicas - 1 + mid_owners), (mid, replicas), (aid, 2 * replicas - 2)):
+
+                @pl.when(phase == which)
+                def _():
+                    pl.semaphore_wait(barrier, count)
+
+            @pl.when(phase == mid)
             def _():
-                others(lambda to: copy_cot(to, me).start())
+                aim_copy.start()
 
         @pl.when(phase == layer)
         def _():
-            aim = target(layer) if layer < top else cot_all[me]
+            aim = target(layer) if layer < mid else (aim_mid[0] if layer == mid else cot_all[me])
             backward = dot_nt(aim, sws[layer][...])
-            grad = 0.5 * (1.0 + bend) + 0.5 * inner * (1.0 - bend * bend) * GELU_A * (
-                1.0 + 3.0 * GELU_B * squared
-            )
-            slope = (grad * backward).astype(BF16)
+            slope = (bent(inner, bend, squared) * backward).astype(BF16)
             if layer == top:
                 slope_all[me] = slope
-                both = jnp.concatenate(
-                    [normed.astype(F32).T, active.astype(F32).T], axis=1
-                ).astype(cols_send.dtype)
-                rows_here = cols_send.shape[1]
-                for d in range(replicas):
-                    cols_send[d] = both[d * rows_here : (d + 1) * rows_here]
+                others(lambda to: copy_back(to, me).start())
+                top_cols(normed, active)
                 cols_all[me] = cols_send[me]
-
-                @others
-                def _(to):
-                    copy_cols(to, me).start()
-                    copy_slope(to, me).start()
-
+            elif layer == mid:
+                mid_start(dot_tn(normed, slope), False)
             else:
                 part = parts[layer]
                 owners, _, rows_here, _ = part.shape
@@ -317,7 +423,26 @@
                     def _():
                         near_copy(layer, w, group_of(layer)[2]).start()
 
-        if layer > 0:
+        if layer == mid:
+
+            @pl.when(phase == helper)
+            def _():
+                aim_copy.wait_recv()
+                mid_start(dot_tn(active, aim_mid[1]), True)
+
+        if layer == top:
+
+            @pl.when(phase == aid)
+            def _():
+                top_cols(normed, active)
+                others(lambda to: copy_cols(to, me).start())
+                top_aim.wait_recv()
+                backward = dot_nt(aim_top[0, 0:cut], sws[layer][...])
+                front = bent(inner[0:cut], bend[0:cut], squared[0:cut]) * backward
+                slope_all[me, 0:cut] = front.astype(BF16)
+                others(lambda to: copy_front(to, me).start())
+
+        elif layer > 0:
             pass_on(layer - 1)
 
         if layer < 3:
@@ -390,7 +515,49 @@
                     :, h * LANES : (h + 1) * LANES
                 ]
 
-    for layer in range(3):
+    @pl.when(phase == helper)
+    def _():
+        mid_each(lambda copy: copy.wait_send(), True)
+
+    @pl.when(phase == aid)
+    def _():
+        @others
+        def _(to):
+            copy_cols(to, me).wait_send()
+            copy_front(to, me).wait_send()
+
+    @pl.when(phase == mid)
+    def _():
+        aim_copy.wait_send()
+        mid_each(lambda copy: copy.wait_send(), False)
+
+        @pl.when(me < mid_owners)
+        def _():
+            got2[me] = part2[me]
+
+            def received(got, recv_sem, sender):
+                if recv_sem is recv_help:
+                    mid_copy(got, recv_sem, 0, sender).wait_recv()
+                else:
+
+                    @pl.when(sender != me)
+                    def _():
+                        mid_copy(got, recv_sem, 0, sender).wait_recv()
+
+                return got[sender].astype(F32)
+
+            for i, (got, recv_sem) in enumerate(((got2, recv_mid), (got_help, recv_help))):
+                total = received(got, recv_sem, 0)
+                if replicas <= 16:
+                    for sender in range(1, replicas):
+                        total = total + received(got, recv_sem, sender)
+                else:
+                    total = lax.fori_loop(
+                        1, replicas, lambda s, t: t + received(got, recv_sem, s), total
+                    )
+                put_grad(mid, i, total)
+
+    for layer in range(2):
         got = gots[layer]
 
         @pl.when(phase == layer)
@@ -422,7 +589,8 @@
             def _():
                 copy_cot(me, sender).wait_recv()
                 copy_cols(me, sender).wait_recv()
-                copy_slope(me, sender).wait_recv()
+                copy_front(me, sender).wait_recv()
+                copy_back(me, sender).wait_recv()
 
             cols = cols_all[sender].astype(BF16)
             return (
@@ -444,8 +612,9 @@
         @others
         def _(to):
             copy_cot(to, me).wait_send()
-            copy_cols(to, me).wait_send()
-            copy_slope(to, me).wait_send()
+            copy_back(to, me).wait_send()
+
+        top_aim.wait_send()
 
 
     for q in range(grad_out.shape[2] // LANES):
@@ -483,6 +652,11 @@
         rows_here = min(widths[layer], owned // widths[layer])
         owners = widths[layer] // rows_here
         kind = narrow(rows_here)
+        if layer == 2:
+            shape = (rows_here, widths[2])
+            parts.append(pltpu.VMEM((owners, *shape), kind))
+            gots.append(pltpu.VMEM((replicas, *shape), kind))
+            break
         parts.append(pltpu.VMEM((owners, 2, rows_here, widths[layer]), kind))
         gots.append(pltpu.VMEM((replicas // owners, 2, rows_here, widths[layer]), kind))
         nears.append(pltpu.VMEM((owners, 2, rows_here, widths[layer]), kind))
@@ -511,6 +685,11 @@
         pltpu.VMEM((replicas, top_rows, 2 * span), narrow(top_rows)),
         pltpu.VMEM((replicas, top_rows, 2 * span), narrow(top_rows)),
         *[sem] * 10,
+        pltpu.VMEM((2, micro * heights[2], widths[2]), BF16),
+        gots[2],
+        *[sem] * 5,
+        pltpu.VMEM((1, span, widths[3]), BF16),
+        *[sem] * 4,
     ]
     held = pl.pallas_call(
         functools.partial(kernel, replicas, heights, widths, micro, len(arrays)),

time: 25.8 us -> 24.8 us (0.961)
  the two profiles are of different devices: /device:TPU:2 before, /device:TPU:3 now
where the time goes in v6:
time: 24.8 us; the launch traced here: 24.6 us
  Pallas kernels  24 us (97%)
  between operations  0.65 us (3%)
    pallas_call x1, Pallas kernels, on_device(): pl.pallas_call(functools.partial(kernel, replicas, heights, widths, micro...  23.2 us
    pallas_call x1, Pallas kernels, on_device(): pl.pallas_call(deliver, out_shape=(jax.ShapeDtypeStruct((1, micro, elemen...  0.73 us

profile of v6, /device:TPU:3, one launch (start us, length us, event | category | flops | bytes accessed | tf_op | source)
XLA Modules:
  0.0 24.6 jit_solution(9664070699653944223)
XLA Ops:
  0.6 23.2 %shard_map.275 = (bf16[1,2,16384]{2,1,0:T(2,128)(2,1)S(1)}, f32[1,2,32768]{2,1,0:T(2,128)S(1)}) custom-call(bf16[2,16384]{1,0:T(2,128)(2,1)} %refs_0_.1, s32[1,2]{1,0:T(1,128)} %bitcast.11, s32[27,2,256]{2,1,0:T(2,128)} %bitcast.6, s32[27,2,128]{2,1,0:T(2,128)} %bitcast.7, s32[27,2,64]{2,1,0:T(2,128)} %bitcast.8, s32[27,2,32]{2,1,0:T(2,128)} %bitcast.9, ...), custom_call_target="tpu_custom_call" | custom-call | tf_op jit(solution)/shard_map/pallas_call | solution.py:694
  23.9 0.7 %shard_map.276 = (bf16[1,2,16384]{2,1,0:T(2,128)(2,1)}, f32[1,2,32768]{2,1,0:T(2,128)}) custom-call(bf16[1,2,16384]{2,1,0:T(2,128)(2,1)S(1)} %get-tuple-element.4.dec_in, f32[1,2,32768]{2,1,0:T(2,128)S(1)} %get-tuple-element.5.grad_in), custom_call_target="tpu_custom_call" | custom-call | tf_op jit(solution)/shard_map/pallas_call | solution.py:707

commit v7 on v6

--- a/solution.py
+++ b/solution.py
@@ -62,8 +62,10 @@
         got2,
         near0,
         near1,
+        near2,
         sum0,
         sum1,
+        sum2,
         cot_all,
         slope_all,
         cols_send,
@@ -84,6 +86,8 @@
         recv_aim,
         send_mid,
         recv_mid,
+        send_far,
+        recv_far,
         recv_help,
         aim_top,
         send_top,
@@ -91,7 +95,7 @@
         send_front,
         recv_front,
     ) = refs
-    nears, sums_of = (near0, near1), (sum0, sum1)
+    nears, sums_of = (near0, near1, near2), (sum0, sum1, sum2)
     features, counts, cot = held[0], held[1], held[27]
     kms, pms, dws = held[2:6], held[6:9], held[9:13]
     fws, sws = held[13:17], held[17:21]
@@ -112,7 +116,7 @@
         load(i).start()
 
     mid, helper, aid = 2, 0, 1
-    cut = cot_all.shape[1] // 2
+    cut = cot_all.shape[1] // 4
     barrier = pltpu.get_barrier_semaphore()
 
     @pl.loop(1, replicas)
@@ -120,6 +124,7 @@
         pl.semaphore_signal(barrier, inc=1, device_id=peer(offset), device_id_type=MESH)
 
     mid_owners = part2.shape[0]
+    mid_groups = replicas // mid_owners
 
     @pl.when(phase == helper)
     def _():
@@ -127,10 +132,13 @@
 
     @pl.when((phase == mid) & (me < mid_owners))
     def _():
-        @pl.loop(0, replicas)
-        def _(to):
+        @pl.loop(0, mid_groups)
+        def _(group):
             pl.semaphore_signal(
-                barrier, inc=1, device_id={"phase": helper, "dp": to}, device_id_type=MESH
+                barrier,
+                inc=1,
+                device_id={"phase": helper, "dp": group * mid_owners + me},
+                device_id_type=MESH,
             )
 
     @pl.when(phase == aid)
@@ -194,7 +202,7 @@
         return top_copy(rows, rows, send_front, recv_front, to, sender)
 
     def copy_back(to, sender):
-        rows = slope_all.at[sender, pl.ds(cut, cut)]
+        rows = slope_all.at[sender, pl.ds(cut, cot_all.shape[1] - cut)]
         return top_copy(rows, rows, send_slope, recv_slope, to, sender)
 
     top_aim = pltpu.make_async_remote_copy(
@@ -255,31 +263,62 @@
         device_id_type=MESH,
     )
 
-    def mid_copy(got, recv_sem, w, sender):
+    def mid_near(w, sender):
+        _, group, _ = group_of(mid)
         return pltpu.make_async_remote_copy(
             src_ref=part2.at[w],
-            dst_ref=got.at[sender],
+            dst_ref=near2.at[sender],
             send_sem=send_mid.at[w],
-            recv_sem=recv_sem.at[sender],
-            device_id={"phase": mid, "dp": w},
+            recv_sem=recv_mid.at[sender],
+            device_id={"phase": phase, "dp": group * mid_owners + w},
             device_id_type=MESH,
         )
 
-    def mid_start(term, helping):
+    def mid_far(got, recv_sem, group):
+        return pltpu.make_async_remote_copy(
+            src_ref=sum2.at[0],
+            dst_ref=got.at[group],
+            send_sem=send_far.at[0],
+            recv_sem=recv_sem.at[group],
+            device_id={"phase": mid, "dp": group_of(mid)[2]},
+            device_id_type=MESH,
+        )
+
+    def mid_start(term):
         rows_here = part2.shape[1]
+        member = group_of(mid)[2]
         for w in range(mid_owners):
             part2[w] = term[w * rows_here : (w + 1) * rows_here].astype(part2.dtype)
-        mid_each(lambda copy: copy.start(), helping)
-
-    def mid_each(act, helping):
         for w in range(mid_owners):
-            if helping:
-                act(mid_copy(got_help, recv_help, w, me))
-            else:
-
-                @pl.when(me != w)
+
+            @pl.when(member != w)
+            def _():
+                mid_near(w, member).start()
+
+    def mid_pass():
+        @pl.when((phase == mid) | (phase == helper))
+        def _():
+            _, group, member = group_of(mid)
+            near2[member] = part2[member]
+            for w in range(mid_owners):
+
+                @pl.when(member != w)
                 def _():
-                    act(mid_copy(got2, recv_mid, w, me))
+                    mid_near(w, member).wait_send()
+                    mid_near(w, w).wait_recv()
+
+            term = near2[0].astype(F32)
+            for w in range(1, mid_owners):
+                term = term + near2[w].astype(F32)
+            sum2[0] = term.astype(near2.dtype)
+
+            @pl.when(phase == helper)
+            def _():
+                mid_far(got_help, recv_help, group).start()
+
+            @pl.when((phase == mid) & (group != 0))
+            def _():
+                mid_far(got2, recv_far, group).start()
 
     def top_cols(normed, active):
         both = jnp.concatenate([normed.astype(F32).T, active.astype(F32).T], axis=1).astype(cols_send.dtype)
@@ -389,7 +428,7 @@
         encoded = (x.astype(F32) + dot(active, sws[layer][...])).astype(BF16)
         encodes.append(encoded)
         if layer == 0:
-            for which, count in ((helper, replicas - 1 + mid_owners), (mid, replicas), (aid, 2 * replicas - 2)):
+            for which, count in ((helper, replicas), (mid, replicas), (aid, 2 * replicas - 2)):
 
                 @pl.when(phase == which)
                 def _():
@@ -410,7 +449,7 @@
                 top_cols(normed, active)
                 cols_all[me] = cols_send[me]
             elif layer == mid:
-                mid_start(dot_tn(normed, slope), False)
+                mid_start(dot_tn(normed, slope))
             else:
                 part = parts[layer]
                 owners, _, rows_here, _ = part.shape
@@ -428,9 +467,10 @@
             @pl.when(phase == helper)
             def _():
                 aim_copy.wait_recv()
-                mid_start(dot_tn(active, aim_mid[1]), True)
+                mid_start(dot_tn(active, aim_mid[1]))
 
         if layer == top:
+            mid_pass()
 
             @pl.when(phase == aid)
             def _():
@@ -515,10 +555,6 @@
                     :, h * LANES : (h + 1) * LANES
                 ]
 
-    @pl.when(phase == helper)
-    def _():
-        mid_each(lambda copy: copy.wait_send(), True)
-
     @pl.when(phase == aid)
     def _():
         @others
@@ -526,36 +562,29 @@
             copy_cols(to, me).wait_send()
             copy_front(to, me).wait_send()
 
+    @pl.when(phase == helper)
+    def _():
+        mid_far(got_help, recv_help, 0).wait_send()
+
     @pl.when(phase == mid)
     def _():
         aim_copy.wait_send()
-        mid_each(lambda copy: copy.wait_send(), False)
-
-        @pl.when(me < mid_owners)
+        group = group_of(mid)[1]
+
+        @pl.when(group != 0)
         def _():
-            got2[me] = part2[me]
-
-            def received(got, recv_sem, sender):
-                if recv_sem is recv_help:
-                    mid_copy(got, recv_sem, 0, sender).wait_recv()
-                else:
-
-                    @pl.when(sender != me)
-                    def _():
-                        mid_copy(got, recv_sem, 0, sender).wait_recv()
-
-                return got[sender].astype(F32)
-
-            for i, (got, recv_sem) in enumerate(((got2, recv_mid), (got_help, recv_help))):
-                total = received(got, recv_sem, 0)
-                if replicas <= 16:
-                    for sender in range(1, replicas):
-                        total = total + received(got, recv_sem, sender)
-                else:
-                    total = lax.fori_loop(
-                        1, replicas, lambda s, t: t + received(got, recv_sem, s), total
-                    )
-                put_grad(mid, i, total)
+            mid_far(got2, recv_far, 0).wait_send()
+
+        @pl.when(group == 0)
+        def _():
+            got2[0] = sum2[0]
+            for i, (got, recv_sem) in enumerate(((got2, recv_far), (got_help, recv_help))):
+                for sender in range(1 - i, mid_groups):
+                    mid_far(got, recv_sem, sender).wait_recv()
+                term = got[0].astype(F32)
+                for sender in range(1, mid_groups):
+                    term = term + got[sender].astype(F32)
+                put_grad(mid, i, term)
 
     for layer in range(2):
         got = gots[layer]
@@ -654,8 +683,8 @@
         kind = narrow(rows_here)
         if layer == 2:
             shape = (rows_here, widths[2])
-            parts.append(pltpu.VMEM((owners, *shape), kind))
-            gots.append(pltpu.VMEM((replicas, *shape), kind))
+            for held, first in ((parts, owners), (gots, replicas // owners), (nears, owners), (sums_of, 1)):
+                held.append(pltpu.VMEM((first, *shape), kind))
             break
         parts.append(pltpu.VMEM((owners, 2, rows_here, widths[layer]), kind))
         gots.append(pltpu.VMEM((replicas // owners, 2, rows_here, widths[layer]), kind))
@@ -687,7 +716,7 @@
         *[sem] * 10,
         pltpu.VMEM((2, micro * heights[2], widths[2]), BF16),
         gots[2],
-        *[sem] * 5,
+        *[sem] * 7,
         pltpu.VMEM((1, span, widths[3]), BF16),
         *[sem] * 4,
     ]

time: 24.8 us -> 22.8 us (0.919)
  the two profiles are of different devices: /device:TPU:3 before, /device:TPU:2 now
where the time goes in v7:
time: 22.8 us; the launch traced here: 22.6 us
  Pallas kernels  22 us (96%)
  between operations  0.65 us (3%)
    pallas_call x1, Pallas kernels, on_device(): pl.pallas_call(functools.partial(kernel, replicas, heights, widths, micro...  21.2 us
    pallas_call x1, Pallas kernels, on_device(): pl.pallas_call(deliver, out_shape=(jax.ShapeDtypeStruct((1, micro, elemen...  0.73 us

profile of v7, /device:TPU:2, one launch (start us, length us, event | category | flops | bytes accessed | tf_op | source)
XLA Modules:
  0.0 22.6 jit_solution(12777873320474415228)
XLA Ops:
  0.6 21.2 %shard_map.275 = (bf16[1,2,16384]{2,1,0:T(2,128)(2,1)S(1)}, f32[1,2,32768]{2,1,0:T(2,128)S(1)}) custom-call(bf16[2,16384]{1,0:T(2,128)(2,1)} %refs_0_.1, s32[1,2]{1,0:T(1,128)} %bitcast.11, s32[27,2,256]{2,1,0:T(2,128)} %bitcast.6, s32[27,2,128]{2,1,0:T(2,128)} %bitcast.7, s32[27,2,64]{2,1,0:T(2,128)} %bitcast.8, s32[27,2,32]{2,1,0:T(2,128)} %bitcast.9, ...), custom_call_target="tpu_custom_call" | custom-call | tf_op jit(solution)/shard_map/pallas_call | solution.py:723
  21.9 0.7 %shard_map.276 = (bf16[1,2,16384]{2,1,0:T(2,128)(2,1)}, f32[1,2,32768]{2,1,0:T(2,128)}) custom-call(bf16[1,2,16384]{2,1,0:T(2,128)(2,1)S(1)} %get-tuple-element.4.dec_in, f32[1,2,32768]{2,1,0:T(2,128)S(1)} %get-tuple-element.5.grad_in), custom_call_target="tpu_custom_call" | custom-call | tf_op jit(solution)/shard_map/pallas_call | solution.py:736

commit v8 on v7

--- a/solution.py
+++ b/solution.py
@@ -32,8 +32,9 @@
 
 
 def one_hot(column, width):
-    lanes = lax.broadcasted_iota(jnp.int32, (column.shape[0], width), 1).astype(F32)
-    return jnp.where(column == lanes, 1.0, 0.0).astype(BF16)
+    lanes = lax.broadcasted_iota(jnp.int32, (column.shape[0], width), 1).astype(F32).astype(BF16)
+    wide = jnp.broadcast_to(column, lanes.shape).astype(BF16)
+    return jnp.where(wide == lanes, jnp.ones_like(lanes), jnp.zeros_like(lanes))
 
 
 def pool_matrix(parent_row, coarse):
@@ -410,13 +411,10 @@
         for start in range(0, micro * rows, group):
             block = x[start : start + group]
             index = idx_t[base[layer] + start : base[layer] + start + group, :]
-            mixed = jnp.zeros((group, width), F32)
-            for first in range(0, TAPS, BATCH):
-                hots = [one_hot(index[:, k : k + 1], group) for k in range(first, first + BATCH)]
-                gathered = dot(jnp.concatenate(hots, axis=0), block)
-                for k in range(BATCH):
-                    tap = dws[layer][first + k : first + k + 1, :].astype(F32)
-                    mixed = mixed + gathered[k * group : (k + 1) * group] * tap
+            taps = dws[layer][...]
+            scaled = jnp.concatenate([block * taps[k : k + 1, :] for k in range(TAPS)], axis=0)
+            hots = jnp.concatenate([one_hot(index[:, k : k + 1], group) for k in range(TAPS)], axis=1)
+            mixed = dot(hots, scaled)
             mixes.append(mixed)
         mixed = mixes[0] if len(mixes) == 1 else jnp.concatenate(mixes, axis=0)
         normed_f = mixed * lax.rsqrt(jnp.mean(mixed * mixed, axis=1, keepdims=True) + 1e-05)

time: 22.8 us -> 22.9 us (level)
  the two profiles are of different devices: /device:TPU:2 before, /device:TPU:6 now
where the time goes in v8:
time: 22.9 us; the launch traced here: 22.7 us
  Pallas kernels  22.1 us (97%)
  between operations  0.65 us (3%)
    pallas_call x1, Pallas kernels, on_device(): pl.pallas_call(functools.partial(kernel, replicas, heights, widths, micro...  21.3 us
    pallas_call x1, Pallas kernels, on_device(): pl.pallas_call(deliver, out_shape=(jax.ShapeDtypeStruct((1, micro, elemen...  0.73 us

profile of v8, /device:TPU:6, one launch (start us, length us, event | category | flops | bytes accessed | tf_op | source)
XLA Modules:
  0.0 22.7 jit_solution(6869958152317580788)
XLA Ops:
  0.6 21.3 %shard_map.275 = (bf16[1,2,16384]{2,1,0:T(2,128)(2,1)S(1)}, f32[1,2,32768]{2,1,0:T(2,128)S(1)}) custom-call(bf16[2,16384]{1,0:T(2,128)(2,1)} %refs_0_.1, s32[1,2]{1,0:T(1,128)} %bitcast.11, s32[27,2,256]{2,1,0:T(2,128)} %bitcast.6, s32[27,2,128]{2,1,0:T(2,128)} %bitcast.7, s32[27,2,64]{2,1,0:T(2,128)} %bitcast.8, s32[27,2,32]{2,1,0:T(2,128)} %bitcast.9, ...), custom_call_target="tpu_custom_call" | custom-call | tf_op jit(solution)/shard_map/pallas_call | solution.py:721
  22.0 0.7 %shard_map.276 = (bf16[1,2,16384]{2,1,0:T(2,128)(2,1)}, f32[1,2,32768]{2,1,0:T(2,128)}) custom-call(bf16[1,2,16384]{2,1,0:T(2,128)(2,1)S(1)} %get-tuple-element.4.dec_in, f32[1,2,32768]{2,1,0:T(2,128)S(1)} %get-tuple-element.5.grad_in), custom_call_target="tpu_custom_call" | custom-call | tf_op jit(solution)/shard_map/pallas_call | solution.py:734

commit v9 on v7

--- a/solution.py
+++ b/solution.py
@@ -32,8 +32,9 @@
 
 
 def one_hot(column, width):
-    lanes = lax.broadcasted_iota(jnp.int32, (column.shape[0], width), 1).astype(F32)
-    return jnp.where(column == lanes, 1.0, 0.0).astype(BF16)
+    lanes = lax.broadcasted_iota(jnp.int32, (column.shape[0], width), 1).astype(F32).astype(BF16)
+    wide = jnp.broadcast_to(column, lanes.shape).astype(BF16)
+    return jnp.where(wide == lanes, jnp.ones_like(lanes), jnp.zeros_like(lanes))
 
 
 def pool_matrix(parent_row, coarse):
@@ -87,7 +88,6 @@
         send_mid,
         recv_mid,
         send_far,
-        recv_far,
         recv_help,
         aim_top,
         send_top,
@@ -284,19 +284,35 @@
             device_id_type=MESH,
         )
 
-    def mid_start(term):
+    def mid_direct(w, sender):
+        return pltpu.make_async_remote_copy(
+            src_ref=part2.at[w],
+            dst_ref=got2.at[sender],
+            send_sem=send_mid.at[w],
+            recv_sem=recv_mid.at[sender],
+            device_id={"phase": mid, "dp": w},
+            device_id_type=MESH,
+        )
+
+    def mid_start(term, helping):
         rows_here = part2.shape[1]
         member = group_of(mid)[2]
         for w in range(mid_owners):
             part2[w] = term[w * rows_here : (w + 1) * rows_here].astype(part2.dtype)
         for w in range(mid_owners):
-
-            @pl.when(member != w)
-            def _():
-                mid_near(w, member).start()
+            if helping:
+
+                @pl.when(member != w)
+                def _():
+                    mid_near(w, member).start()
+            else:
+
+                @pl.when(me != w)
+                def _():
+                    mid_direct(w, me).start()
 
     def mid_pass():
-        @pl.when((phase == mid) | (phase == helper))
+        @pl.when(phase == helper)
         def _():
             _, group, member = group_of(mid)
             near2[member] = part2[member]
@@ -312,13 +328,7 @@
                 term = term + near2[w].astype(F32)
             sum2[0] = term.astype(near2.dtype)
 
-            @pl.when(phase == helper)
-            def _():
-                mid_far(got_help, recv_help, group).start()
-
-            @pl.when((phase == mid) & (group != 0))
-            def _():
-                mid_far(got2, recv_far, group).start()
+            mid_far(got_help, recv_help, group).start()
 
     def top_cols(normed, active):
         both = jnp.concatenate([normed.astype(F32).T, active.astype(F32).T], axis=1).astype(cols_send.dtype)
@@ -449,7 +459,7 @@
                 top_cols(normed, active)
                 cols_all[me] = cols_send[me]
             elif layer == mid:
-                mid_start(dot_tn(normed, slope))
+                mid_start(dot_tn(normed, slope), False)
             else:
                 part = parts[layer]
                 owners, _, rows_here, _ = part.shape
@@ -467,7 +477,7 @@
             @pl.when(phase == helper)
             def _():
                 aim_copy.wait_recv()
-                mid_start(dot_tn(active, aim_mid[1]))
+                mid_start(dot_tn(active, aim_mid[1]), True)
 
         if layer == top:
             mid_pass()
@@ -569,22 +579,37 @@
     @pl.when(phase == mid)
     def _():
         aim_copy.wait_send()
-        group = group_of(mid)[1]
-
-        @pl.when(group != 0)
+
+        for w in range(mid_owners):
+
+            @pl.when(me != w)
+            def _():
+                mid_direct(w, me).wait_send()
+
+        @pl.when(me < mid_owners)
         def _():
-            mid_far(got2, recv_far, 0).wait_send()
-
-        @pl.when(group == 0)
-        def _():
-            got2[0] = sum2[0]
-            for i, (got, recv_sem) in enumerate(((got2, recv_far), (got_help, recv_help))):
-                for sender in range(1 - i, mid_groups):
-                    mid_far(got, recv_sem, sender).wait_recv()
-                term = got[0].astype(F32)
-                for sender in range(1, mid_groups):
-                    term = term + got[sender].astype(F32)
-                put_grad(mid, i, term)
+            got2[me] = part2[me]
+
+            def received(sender):
+                @pl.when(sender != me)
+                def _():
+                    mid_direct(0, sender).wait_recv()
+
+                return got2[sender].astype(F32)
+
+            total = received(0)
+            if replicas <= 16:
+                for sender in range(1, replicas):
+                    total = total + received(sender)
+            else:
+                total = lax.fori_loop(1, replicas, lambda s, t: t + received(s), total)
+            put_grad(mid, 0, total)
+            for sender in range(mid_groups):
+                mid_far(got_help, recv_help, sender).wait_recv()
+            term = got_help[0].astype(F32)
+            for sender in range(1, mid_groups):
+                term = term + got_help[sender].astype(F32)
+            put_grad(mid, 1, term)
 
     for layer in range(2):
         got = gots[layer]
@@ -683,7 +708,7 @@
         kind = narrow(rows_here)
         if layer == 2:
             shape = (rows_here, widths[2])
-            for held, first in ((parts, owners), (gots, replicas // owners), (nears, owners), (sums_of, 1)):
+            for held, first in ((parts, owners), (gots, replicas), (nears, owners), (sums_of, 1)):
                 held.append(pltpu.VMEM((first, *shape), kind))
             break
         parts.append(pltpu.VMEM((owners, 2, rows_here, widths[layer]), kind))
@@ -716,7 +741,7 @@
         *[sem] * 10,
         pltpu.VMEM((2, micro * heights[2], widths[2]), BF16),
         gots[2],
-        *[sem] * 7,
+        *[sem] * 6,
         pltpu.VMEM((1, span, widths[3]), BF16),
         *[sem] * 4,
     ]

time: 22.8 us -> 21.9 us (0.961)
  the two profiles are of different devices: /device:TPU:2 before, /device:TPU:0 now
where the time goes in v9:
time: 21.9 us; the launch traced here: 21.8 us
  Pallas kernels  21.1 us (96%)
  between operations  0.65 us (3%)
    pallas_call x1, Pallas kernels, on_device(): pl.pallas_call(functools.partial(kernel, replicas, heights, widths, micro...  20.4 us
    pallas_call x1, Pallas kernels, on_device(): pl.pallas_call(deliver, out_shape=(jax.ShapeDtypeStruct((1, micro, elemen...  0.73 us

profile of v9, /device:TPU:0, one launch (start us, length us, event | category | flops | bytes accessed | tf_op | source)
XLA Modules:
  0.0 21.8 jit_solution(8086487076911946749)
XLA Ops:
  0.6 20.4 %shard_map.275 = (bf16[1,2,16384]{2,1,0:T(2,128)(2,1)S(1)}, f32[1,2,32768]{2,1,0:T(2,128)S(1)}) custom-call(bf16[2,16384]{1,0:T(2,128)(2,1)} %refs_0_.1, s32[1,2]{1,0:T(1,128)} %bitcast.11, s32[27,2,256]{2,1,0:T(2,128)} %bitcast.6, s32[27,2,128]{2,1,0:T(2,128)} %bitcast.7, s32[27,2,64]{2,1,0:T(2,128)} %bitcast.8, s32[27,2,32]{2,1,0:T(2,128)} %bitcast.9, ...), custom_call_target="tpu_custom_call" | custom-call | tf_op jit(solution)/shard_map/pallas_call | solution.py:748
  21.0 0.7 %shard_map.276 = (bf16[1,2,16384]{2,1,0:T(2,128)(2,1)}, f32[1,2,32768]{2,1,0:T(2,128)}) custom-call(bf16[1,2,16384]{2,1,0:T(2,128)(2,1)S(1)} %get-tuple-element.4.dec_in, f32[1,2,32768]{2,1,0:T(2,128)S(1)} %get-tuple-element.5.grad_in), custom_call_target="tpu_custom_call" | custom-call | tf_op jit(solution)/shard_map/pallas_call | solution.py:761

commit v10 on v9

--- a/solution.py
+++ b/solution.py
@@ -420,13 +420,10 @@
         for start in range(0, micro * rows, group):
             block = x[start : start + group]
             index = idx_t[base[layer] + start : base[layer] + start + group, :]
-            mixed = jnp.zeros((group, width), F32)
-            for first in range(0, TAPS, BATCH):
-                hots = [one_hot(index[:, k : k + 1], group) for k in range(first, first + BATCH)]
-                gathered = dot(jnp.concatenate(hots, axis=0), block)
-                for k in range(BATCH):
-                    tap = dws[layer][first + k : first + k + 1, :].astype(F32)
-                    mixed = mixed + gathered[k * group : (k + 1) * group] * tap
+            taps = dws[layer][...]
+            scaled = jnp.concatenate([block * taps[k : k + 1, :] for k in range(TAPS)], axis=0)
+            hots = jnp.concatenate([one_hot(index[:, k : k + 1], group) for k in range(TAPS)], axis=1)
+            mixed = dot(hots, scaled)
             mixes.append(mixed)
         mixed = mixes[0] if len(mixes) == 1 else jnp.concatenate(mixes, axis=0)
         normed_f = mixed * lax.rsqrt(jnp.mean(mixed * mixed, axis=1, keepdims=True) + 1e-05)

time: 21.9 us -> 21.8 us (level)
  no operation moved by 1% of the time
where the time goes in v10:
time: 21.8 us; the launch traced here: 21.6 us
  Pallas kernels  21 us (96%)
  between operations  0.65 us (3%)
    pallas_call x1, Pallas kernels, on_device(): pl.pallas_call(functools.partial(kernel, replicas, heights, widths, micro...  20.2 us
    pallas_call x1, Pallas kernels, on_device(): pl.pallas_call(deliver, out_shape=(jax.ShapeDtypeStruct((1, micro, elemen...  0.73 us

profile of v10, /device:TPU:0, one launch (start us, length us, event | category | flops | bytes accessed | tf_op | source)
XLA Modules:
  0.0 21.6 jit_solution(8822650789339308950)
XLA Ops:
  0.6 20.2 %shard_map.275 = (bf16[1,2,16384]{2,1,0:T(2,128)(2,1)S(1)}, f32[1,2,32768]{2,1,0:T(2,128)S(1)}) custom-call(bf16[2,16384]{1,0:T(2,128)(2,1)} %refs_0_.1, s32[1,2]{1,0:T(1,128)} %bitcast.11, s32[27,2,256]{2,1,0:T(2,128)} %bitcast.6, s32[27,2,128]{2,1,0:T(2,128)} %bitcast.7, s32[27,2,64]{2,1,0:T(2,128)} %bitcast.8, s32[27,2,32]{2,1,0:T(2,128)} %bitcast.9, ...), custom_call_target="tpu_custom_call" | custom-call | tf_op jit(solution)/shard_map/pallas_call | solution.py:745
  20.9 0.7 %shard_map.276 = (bf16[1,2,16384]{2,1,0:T(2,128)(2,1)}, f32[1,2,32768]{2,1,0:T(2,128)}) custom-call(bf16[1,2,16384]{2,1,0:T(2,128)(2,1)S(1)} %get-tuple-element.4.dec_in, f32[1,2,32768]{2,1,0:T(2,128)S(1)} %get-tuple-element.5.grad_in), custom_call_target="tpu_custom_call" | custom-call | tf_op jit(solution)/shard_map/pallas_call | solution.py:758
